TPU v7x, 32 devices: a whole 2x2x4 slice. The times are simulated.
32 devices in a mesh: gx: 8 (over y, x, core), sa: 4 (over z).
Axes of the slice: x: 2, y: 2, z: 4, core: 2. Of those that a mesh axis runs over, the one named last changes fastest.
Arguments:
- scan_feats: bfloat16 [96, 2048, 128], P(None, ('gx', 'sa')), may hold values from -6 to 6
- row_owner: int32 [2048], P(('gx', 'sa')), may hold values from 0 to 31, as said below
- row_voxels: int32 [2048, 128], P(('gx', 'sa')), may hold values from 0 to 511, as said below
- row_count: int32 [2048], P(('gx', 'sa')), may hold values from 1 to 128, as said below
- occupancy: int32 [16, 1024], P('gx', 'sa'), may hold values 0 or 1
- weight_one: bfloat16 [27, 96, 96], replicated, may hold values from -0.125 to 0.125
- weight_two: bfloat16 [27, 96, 96], replicated, may hold values from -0.125 to 0.125
- cotangent: bfloat16 [96, 16, 1024], P(None, 'gx', 'sa'), may hold values from -6 to 6
Outputs:
- out_field: bfloat16 [96, 16, 1024], P(None, 'gx', 'sa')
- grad_scan: bfloat16 [96, 2048, 128], P(None, ('gx', 'sa'))
- grad_w1: float32 [27, 96, 96], replicated
- grad_w2: float32 [27, 96, 96], replicated
Inputs may be any that keep to these rules, and one draw needn't show every extreme that they name: `row_owner`: in each device's block of 64 rows no owner is named by more than 4 rows, and one owner, the same for all blocks, is named by exactly 4 rows in every block. `row_count`: the first row of each device's block lists 128 voxels. `row_voxels`: within a row the listed positions are distinct; positions at slots beyond the row's count are not used.
All inputs are finite; a program needn't handle non-finite values. No bound on the sum of `occupancy` on one device may be relied on, other than what follows from the above.
Results may differ from a plain program's by a relative error of at most 0.0058.
Values may be sent and summed in bfloat16 or wider, within the bound.
A program may use at most 128 MiB of HBM per device.

v0:
```python
import math

import jax
import jax.numpy as jnp
from jax import lax
from jax.sharding import PartitionSpec as P

EDGE = 16


def with_halo(cells, sides, width):
    for axis, dim in sides:
        count = lax.axis_size(axis)
        ends = count - 1
        head = lax.slice_in_dim(cells, 0, width, axis=dim)
        tail = lax.slice_in_dim(cells, cells.shape[dim] - width, cells.shape[dim], axis=dim)
        cells = jnp.concatenate(
            [
                lax.ppermute(tail, axis, [(i, (i + 1) % count) for i in range(ends)]),
                cells,
                lax.ppermute(head, axis, [((i + 1) % count, i) for i in range(ends)]),
            ],
            axis=dim,
        )
    return cells


def span_limits(slab_len, brick_edge):
    side_len = brick_edge + 2
    plane_len = side_len * side_len
    first_cell = plane_len + side_len + 1
    return (first_cell, (slab_len + 2) * plane_len - 2 * first_cell)


def extend(field):
    channels, slab_len, plane_len = field.shape
    brick_edge = EDGE
    x_extended = with_halo(field, (("gx", 1),), 1)
    xy_extended = with_halo(x_extended, (("sa", 2),), brick_edge)
    cube_view = xy_extended.reshape(channels, slab_len + 2, brick_edge + 2, brick_edge)
    cube_view = jnp.pad(cube_view, ((0, 0), (0, 0), (0, 0), (1, 1)))
    return cube_view.reshape(channels, -1)


def interior(running, slab_len, brick_edge):
    channels = running.shape[0]
    side_len = brick_edge + 2
    first_cell, span_len = span_limits(slab_len, brick_edge)
    padded = jnp.pad(running, ((0, 0), (first_cell, first_cell)))
    cube_view = padded.reshape(channels, slab_len + 2, side_len, side_len)[:, 1:-1, 1:-1, 1:-1]
    return cube_view.reshape(channels, slab_len, brick_edge * brick_edge)


def embed_span(field, slab_len, brick_edge):
    channels = field.shape[0]
    first_cell, span_len = span_limits(slab_len, brick_edge)
    cube_view = field.reshape(channels, slab_len, brick_edge, brick_edge)
    padded = jnp.pad(cube_view, ((0, 0), (1, 1), (1, 1), (1, 1))).reshape(channels, -1)
    return lax.slice_in_dim(padded, first_cell, first_cell + span_len, axis=1)


def offset_slice(extended, offset_k, slab_len, brick_edge):
    side_len = brick_edge + 2
    plane_len = side_len * side_len
    first_cell, span_len = span_limits(slab_len, brick_edge)
    shift_x = offset_k // 9
    shift_y = offset_k // 3 % 3
    shift_z = offset_k % 3
    begin = first_cell + (shift_x - 1) * plane_len + (shift_y - 1) * side_len + shift_z - 1
    return lax.slice_in_dim(extended, begin, begin + span_len, axis=1)


def convolve(extended, weight, slab_len, brick_edge):
    running = None
    for offset_k in range(27):
        piece = offset_slice(extended, offset_k, slab_len, brick_edge)
        term = lax.dot_general(
            weight[offset_k], piece, (((0,), (0,)), ((), ())), preferred_element_type=jnp.float32
        )
        running = term if running is None else running + term
    return interior(running, slab_len, brick_edge)


def weight_grad(extended, grad_span, slab_len, brick_edge):
    products = []
    for offset_k in range(27):
        piece = offset_slice(extended, offset_k, slab_len, brick_edge)
        products.append(
            lax.dot_general(
                piece, grad_span, (((1,), (1,)), ((), ())), preferred_element_type=jnp.float32
            )
        )
    return jnp.stack(products, axis=0)


def mirrored(weight):
    return jnp.transpose(weight[::-1], (0, 2, 1))


def on_device(
    scan_feats, row_owner, row_voxels, row_count, occupancy, weight_one, weight_two, cotangent
):
    channels, row_total, slot_len = scan_feats.shape
    slab_len = occupancy.shape[0]
    brick_edge = EDGE
    gx_count = lax.axis_size("gx")
    sa_count = lax.axis_size("sa")
    devices = gx_count * sa_count
    capacity = max(2, 2 * row_total // devices)
    send_rows = devices * capacity
    cell_total = slab_len * brick_edge * brick_edge
    row_order = jnp.arange(row_total)
    earlier = (row_owner[:, None] == row_owner[None, :]) & (row_order[None, :] < row_order[:, None])
    slot_rank = jnp.sum(earlier.astype(jnp.int32), axis=1)
    target = row_owner * capacity + slot_rank
    is_live = jnp.arange(slot_len)[None, :] < row_count[:, None]
    live_feats = jnp.where(is_live[None], scan_feats, jnp.zeros((), scan_feats.dtype))
    live_places = jnp.where(is_live, row_voxels, -1)
    place_match = target[None, :] == jnp.arange(send_rows)[:, None]
    place_bf = place_match.astype(jnp.bfloat16)
    send_feats = jnp.einsum(
        "crs,tr->cts", live_feats, place_bf, preferred_element_type=jnp.float32
    ).astype(jnp.bfloat16)
    shifted_places = (live_places + 1).astype(jnp.float32)
    send_float = jnp.einsum(
        "rs,tr->ts",
        shifted_places,
        place_match.astype(jnp.float32),
        precision=lax.Precision.HIGHEST,
    )
    send_places = (send_float.astype(jnp.int32) - 1)[None]
    got_feats, got_places = (
        lax.all_to_all(
            send_feats.reshape(channels, devices, capacity, slot_len),
            ("gx", "sa"),
            split_axis=1,
            concat_axis=1,
            tiled=True,
        ),
        lax.all_to_all(
            send_places.reshape(1, devices, capacity, slot_len),
            ("gx", "sa"),
            split_axis=1,
            concat_axis=1,
            tiled=True,
        ),
    )
    flat_places = got_places.reshape(-1)
    flat_feats = got_feats.reshape(channels, -1)
    index_total = flat_places.shape[0]
    block_len = math.gcd(index_total, max(slot_len, (1 << 22) // cell_total))
    block_starts = jnp.arange(0, index_total, block_len)
    cell_ids = jnp.arange(cell_total)

    def add_block(running, offset_at):
        block_places = lax.dynamic_slice_in_dim(flat_places, offset_at, block_len)
        block_feats = lax.dynamic_slice_in_dim(flat_feats, offset_at, block_len, 1)
        one_hot = (block_places[:, None] == cell_ids[None, :]).astype(jnp.bfloat16)
        return (running + jnp.dot(block_feats, one_hot, preferred_element_type=jnp.float32), None)

    summed, unused_out = lax.scan(
        add_block, jnp.zeros((channels, cell_total), jnp.float32), block_starts
    )
    occupied = occupancy.astype(jnp.float32)[None]
    voxels_in = (occupied * summed.reshape(channels, slab_len, brick_edge * brick_edge)).astype(
        jnp.bfloat16
    )
    input_ext = extend(voxels_in)
    first_pre = convolve(input_ext, weight_one, slab_len, brick_edge)
    hidden = (occupied * jax.nn.silu(first_pre)).astype(jnp.bfloat16)
    hidden_ext = extend(hidden)
    second_pre = convolve(hidden_ext, weight_two, slab_len, brick_edge)
    out_field = (occupied * second_pre).astype(jnp.bfloat16)
    grad_out = jnp.where(occupancy[None] > 0, cotangent, jnp.zeros((), cotangent.dtype))
    part_two = weight_grad(
        hidden_ext, embed_span(grad_out, slab_len, brick_edge), slab_len, brick_edge
    )
    grad_hidden = convolve(extend(grad_out), mirrored(weight_two), slab_len, brick_edge)
    sigmoid_first = jax.nn.sigmoid(first_pre)
    silu_slope = sigmoid_first * (1.0 + first_pre * (1.0 - sigmoid_first))
    grad_first = (occupied * grad_hidden * silu_slope).astype(jnp.bfloat16)
    part_one = weight_grad(
        input_ext, embed_span(grad_first, slab_len, brick_edge), slab_len, brick_edge
    )
    grad_voxels = convolve(extend(grad_first), mirrored(weight_one), slab_len, brick_edge)
    grad_cells = (occupied * grad_voxels).astype(jnp.bfloat16).reshape(channels, -1)

    def pick_block(offset_at):
        block_places = lax.dynamic_slice_in_dim(flat_places, offset_at, block_len)
        one_hot = (block_places[:, None] == cell_ids[None, :]).astype(jnp.bfloat16)
        picked = lax.dot_general(
            grad_cells, one_hot, (((1,), (1,)), ((), ())), preferred_element_type=jnp.float32
        )
        return picked.astype(jnp.bfloat16)

    picked_blocks = lax.map(pick_block, block_starts)
    returned = jnp.moveaxis(picked_blocks, 1, 0).reshape((channels,) + got_places.shape[1:])
    arrived = lax.all_to_all(returned, ("gx", "sa"), split_axis=1, concat_axis=1, tiled=True)
    arrived = arrived.reshape(channels, send_rows, slot_len)
    own_rows = jnp.einsum(
        "cts,tr->crs", arrived, place_bf, preferred_element_type=jnp.float32
    ).astype(jnp.bfloat16)
    grad_scan = jnp.where(is_live[None], own_rows, jnp.zeros((), jnp.bfloat16))
    total_one, total_two = lax.psum((part_one, part_two), ("gx", "sa"))
    factor = 1.0 / math.sqrt(slab_len * brick_edge * brick_edge * devices)
    return (out_field, grad_scan, total_one * factor, total_two * factor)


def solution(mesh):
    return jax.shard_map(
        on_device,
        mesh=mesh,
        in_specs=(
            P(None, ("gx", "sa"), None),
            P(("gx", "sa")),
            P(("gx", "sa"), None),
            P(("gx", "sa")),
            P("gx", "sa"),
            P(),
            P(),
            P(None, "gx", "sa"),
        ),
        out_specs=(P(None, "gx", "sa"), P(None, ("gx", "sa"), None), P(), P()),
        check_vma=False,
    )
```

profile of v0, /device:TPU:0, one launch (start us, length us, event | category | flops | bytes accessed | tf_op | source)
XLA Modules:
  0.0 447.6 jit_solution(139735717484668820)
XLA Ops:
  21.6 7.9 %all-to-all-start = ((bf16[96,32,4,128]{3,2,0,1:T(4,128)(2,1)}), bf16[96,32,4,128]{3,2,0,1:T(4,128)(2,1)S(1)}, u32[]{:S(2)}, u32[]{:S(2)}) async-start(bf16[96,32,4,128]{3,2,0,1:T(4,128)(2,1)} %copy.48), calls=%async_computation | async-start | bytes 6291456 | tf_op jit(solution)/shard_map/all_to_all | solution.py:133
  35.3 4.5 %collective-permute-start.10 = (bf16[96,4,16]{0,2,1:T(8,128)(2,1)S(1)}, bf16[96,4,16]{0,2,1:T(8,128)(2,1)S(1)}, u32[]{:S(2)}, u32[]{:S(2)}) collective-permute-start(bf16[96,4,16]{0,2,1:T(8,128)(2,1)S(1)} %get-tuple-element.167), channel_id=1, source_target_pairs={{0,1},{1,2},{2,3},{4,5},{5,6},{6,7},{8,9},{9,10},{10,11},{12,13},{... | collective-permute-start | bytes 36872 | tf_op jit(solution)/shard_map/ppermute | solution.py:19
  44.4 21.0 %collective-permute-done.11 = bf16[96,4,16]{0,2,1:T(8,128)(2,1)S(1)} collective-permute-done((bf16[96,4,16]{0,2,1:T(8,128)(2,1)S(1)}, bf16[96,4,16]{0,2,1:T(8,128)(2,1)S(1)}, u32[]{:S(2)}, u32[]{:S(2)}) %collective-permute-start.11) | collective-permute-done | bytes 12320 | tf_op jit(solution)/shard_map/ppermute | solution.py:21
  65.4 16.1 %collective-permute-done.10 = bf16[96,4,16]{0,2,1:T(8,128)(2,1)S(1)} collective-permute-done((bf16[96,4,16]{0,2,1:T(8,128)(2,1)S(1)}, bf16[96,4,16]{0,2,1:T(8,128)(2,1)S(1)}, u32[]{:S(2)}, u32[]{:S(2)}) %collective-permute-start.10) | collective-permute-done | bytes 12320 | tf_op jit(solution)/shard_map/ppermute | solution.py:19
  99.7 19.9 %all-to-all-start.1 = ((s32[1,32,4,128]{3,2,0,1:T(4,128)}), s32[1,32,4,128]{3,2,0,1:T(4,128)S(1)}, u32[]{:S(2)}, u32[]{:S(2)}) async-start(s32[1,32,4,128]{3,2,0,1:T(4,128)} %bitcast.822), calls=%async_computation.1 | async-start | bytes 131072 | tf_op jit(solution)/shard_map/all_to_all | solution.py:140
  121.2 3.4 copy.49
  124.7 4.8 %reshape.116 = bf16[96,16384]{1,0:T(8,128)(2,1)S(1)} reshape(bf16[96,32,4,128]{3,2,1,0:T(4,128)(2,1)} %copy.49) | data formatting | bytes 6291456 | tf_op jit(solution)/shard_map/reshape | solution.py:149
  129.4 18.4 %while.23 = (s32[]{:T(128)}, f32[96,512]{1,0:T(8,128)}, s32[2]{0:T(128)}, bf16[96,16384]{1,0:T(8,128)(2,1)S(1)}, s32[16384]{0:T(1024)S(1)}, /*index=5*/s32[]{:T(128)}, s32[]{:T(128)}, s32[]{:T(128)}) while((s32[]{:T(128)}, f32[96,512]{1,0:T(8,128)}, s32[2]{0:T(128)}, bf16[96,16384]{1,0:T(8,128)(2,1)S(1)}, s32[16384]{0:T(1024)S(1)}, ...), condition=%wide.region_2.3_spmd.clone, body=%wide.region_1.2_spmd.clone.sunk | while | flops 809598976 | bytes 2064541 | solution.py:161
  133.3 5.3 %fusion.485 = f32[96,512]{1,0:T(8,128)} fusion(s32[8192]{0:T(1024)} %dynamic_slice.34, bf16[96,16384]{1,0:T(8,128)(2,1)S(1)} %get-tuple-element.266, s32[]{:T(128)S(6)} %select_n.43, f32[96,512]{1,0:T(8,128)} %get-tuple-element.256, pred[]{:T(512)S(6)} %compare.13), kind=kOutput, calls=%fused_computation.12.clone.1 | convolution fusion | flops 809598976 | bytes 1998853 | tf_op jit(solution)/shard_map/while/body/eval_jaxpr/dot_general | solution.py:159
  142.4 5.5 %fusion.485 = f32[96,512]{1,0:T(8,128)} fusion(s32[8192]{0:T(1024)} %dynamic_slice.34, bf16[96,16384]{1,0:T(8,128)(2,1)S(1)} %get-tuple-element.266, s32[]{:T(128)S(6)} %select_n.43, f32[96,512]{1,0:T(8,128)} %get-tuple-element.256, pred[]{:T(512)S(6)} %compare.13), kind=kOutput, calls=%fused_computation.12.clone.1 | convolution fusion | flops 809598976 | bytes 1998853 | tf_op jit(solution)/shard_map/while/body/eval_jaxpr/dot_general | solution.py:159
  155.8 4.5 %collective-permute-start.2 = (bf16[96,4,16]{0,2,1:T(8,128)(2,1)S(1)}, bf16[96,4,16]{0,2,1:T(8,128)(2,1)S(1)}, u32[]{:S(2)}, u32[]{:S(2)}) collective-permute-start(bf16[96,4,16]{0,2,1:T(8,128)(2,1)S(1)} %get-tuple-element.171), channel_id=1, source_target_pairs={{0,1},{1,2},{2,3},{4,5},{5,6},{6,7},{8,9},{9,10},{10,11},{12,13},{... | collective-permute-start | bytes 36872 | tf_op jit(solution)/shard_map/ppermute | solution.py:19
  173.7 3.9 collective-permute-start.4
  179.0 5.5 %collective-permute-start.12 = (bf16[96,1,256]{0,2,1:T(8,128)(2,1)S(1)}, bf16[96,1,256]{0,2,1:T(8,128)(2,1)S(1)}, u32[]{:S(2)}, u32[]{:S(2)}) collective-permute-start(bf16[96,1,256]{0,2,1:T(8,128)(2,1)S(1)} %get-tuple-element.173), channel_id=1, source_target_pairs={{0,4},{4,8},{8,12},{12,16},{16,20},{20,24},{24,28},{1,5},{5,9},{9,... | collective-permute-start | bytes 147464 | tf_op jit(solution)/shard_map/ppermute | solution.py:19
  192.4 4.5 %collective-permute-start.6 = (bf16[96,4,16]{0,2,1:T(8,128)(2,1)S(1)}, bf16[96,4,16]{0,2,1:T(8,128)(2,1)S(1)}, u32[]{:S(2)}, u32[]{:S(2)}) collective-permute-start(bf16[96,4,16]{0,2,1:T(8,128)(2,1)S(1)} %get-tuple-element.169), channel_id=1, source_target_pairs={{0,1},{1,2},{2,3},{4,5},{5,6},{6,7},{8,9},{9,10},{10,11},{12,13},{... | collective-permute-start | bytes 36872 | tf_op jit(solution)/shard_map/ppermute | solution.py:19
  198.3 4.8 %collective-permute-start.14 = (bf16[96,4,16]{0,2,1:T(8,128)(2,1)S(1)}, bf16[96,4,16]{0,2,1:T(8,128)(2,1)S(1)}, u32[]{:S(2)}, u32[]{:S(2)}) collective-permute-start(bf16[96,4,16]{0,2,1:T(8,128)(2,1)S(1)} %get-tuple-element.165), channel_id=1, source_target_pairs={{0,1},{1,2},{2,3},{4,5},{5,6},{6,7},{8,9},{9,10},{10,11},{12,13},{... | collective-permute-start | bytes 36872 | tf_op jit(solution)/shard_map/ppermute | solution.py:19
  217.2 15.2 %while.22 = (s32[]{:T(128)}, bf16[2,96,8192]{2,1,0:T(8,128)(2,1)}, s32[2]{0:T(128)S(1)}, s32[16384]{0:T(1024)S(1)}, bf16[96,512]{1,0:T(8,128)(2,1)S(1)}, /*index=5*/s32[]{:T(128)}, s32[]{:T(128)}, s32[]{:T(128)}) while((s32[]{:T(128)}, bf16[2,96,8192]{2,1,0:T(8,128)(2,1)}, s32[2]{0:T(128)S(1)}, s32[16384]{0:T(1024)S(1)}, ...), condition=%wide.region_4.5_spmd.clone, body=%wide.region_3.4_spmd.clone.sunk | while | flops 810287104 | bytes 1769619 | solution.py:196
  219.9 5.0 %fusion.483 = bf16[2,96,8192]{2,1,0:T(8,128)(2,1)} fusion(bf16[2,96,8192]{2,1,0:T(8,128)(2,1)} %get-tuple-element.280, s32[]{:T(128)S(6)} %copy.76, bf16[96,512]{1,0:T(8,128)(2,1)S(1)} %get-tuple-element.291, s32[8192]{0:T(1024)S(1)} %dynamic_slice.31), kind=kOutput, calls=%fused_computation.6.clone.1 | convolution fusion | flops 810287104 | bytes 1703940 | tf_op jit(solution)/shard_map/while/body/eval_jaxpr/dot_general | solution.py:191
  227.4 5.0 %fusion.483 = bf16[2,96,8192]{2,1,0:T(8,128)(2,1)} fusion(bf16[2,96,8192]{2,1,0:T(8,128)(2,1)} %get-tuple-element.280, s32[]{:T(128)S(6)} %copy.76, bf16[96,512]{1,0:T(8,128)(2,1)S(1)} %get-tuple-element.291, s32[8192]{0:T(1024)S(1)} %dynamic_slice.31), kind=kOutput, calls=%fused_computation.6.clone.1 | convolution fusion | flops 810287104 | bytes 1703940 | tf_op jit(solution)/shard_map/while/body/eval_jaxpr/dot_general | solution.py:191
  232.4 5.2 %copy.58 = bf16[96,2,8192]{2,1,0:T(2,128)(2,1)S(1)} copy(bf16[96,2,8192]{2,0,1:T(8,128)(2,1)} %bitcast.815) | data formatting | bytes 6291456 | tf_op jit(solution)/shard_map/transpose | solution.py:197
  237.6 4.0 reshape.135
  241.6 5.1 %copy.59 = bf16[96,32,4,128]{3,2,0,1:T(4,128)(2,1)} copy(bf16[96,32,4,128]{3,2,1,0:T(4,128)(2,1)} %reshape.135) | data formatting | bytes 6291456 | tf_op jit(solution)/shard_map/reshape | solution.py:197
  246.7 6.7 %all-to-all-start.2 = ((bf16[96,32,4,128]{3,2,0,1:T(4,128)(2,1)}), bf16[96,32,4,128]{3,2,0,1:T(4,128)(2,1)S(1)}, u32[]{:S(2)}, u32[]{:S(2)}) async-start(bf16[96,32,4,128]{3,2,0,1:T(4,128)(2,1)} %copy.59), calls=%async_computation.2 | async-start | bytes 6291456 | tf_op jit(solution)/shard_map/all_to_all | solution.py:198
  294.2 139.2 %all-reduce.13.cloned.1.call-done = (f32[27,96,96]{2,1,0:T(8,128)}, f32[27,96,96]{2,1,0:T(8,128)}) async-done(((f32[27,96,96]{2,1,0:T(8,128)}, f32[27,96,96]{2,1,0:T(8,128)}), (f32[27,96,96]{2,1,0:T(8,128)}, f32[27,96,96]{2,1,0:T(8,128)})) %all-reduce.13.cloned.1.call-update) | async-done | bytes 1990672 | tf_op jit(solution)/shard_map/psum | solution.py:204
  433.4 3.4 broadcast_multiply_fusion
  (320 shorter events, 138.4 us)
Async XLA Ops:
  9.0 24.9 %collective-permute-start.9 = (bf16[96,1,256]{0,2,1:T(8,128)(2,1)S(1)}, bf16[96,1,256]{0,2,1:T(8,128)(2,1)S(1)}, u32[]{:S(2)}, u32[]{:S(2)}) collective-permute-start(bf16[96,1,256]{0,2,1:T(8,128)(2,1)S(1)} %get-tuple-element.176), channel_id=1, source_target_pairs={{4,0},{8,4},{12,8},{16,12},{20,16},{24,20},{28,24},{5,1},{9,5},{13... | collective-permute-start | bytes 147464 | tf_op jit(solution)/shard_map/ppermute | solution.py:21
  10.3 23.6 %collective-permute-start.8 = (bf16[96,1,256]{0,2,1:T(8,128)(2,1)S(1)}, bf16[96,1,256]{0,2,1:T(8,128)(2,1)S(1)}, u32[]{:S(2)}, u32[]{:S(2)}) collective-permute-start(bf16[96,1,256]{0,2,1:T(8,128)(2,1)S(1)} %get-tuple-element.175), channel_id=1, source_target_pairs={{0,4},{4,8},{8,12},{12,16},{16,20},{20,24},{24,28},{1,5},{5,9},{9,... | collective-permute-start | bytes 147464 | tf_op jit(solution)/shard_map/ppermute | solution.py:19
  21.6 78.1 %all-to-all-start = ((bf16[96,32,4,128]{3,2,0,1:T(4,128)(2,1)}), bf16[96,32,4,128]{3,2,0,1:T(4,128)(2,1)S(1)}, u32[]{:S(2)}, u32[]{:S(2)}) async-start(bf16[96,32,4,128]{3,2,0,1:T(4,128)(2,1)} %copy.48), calls=%async_computation | async-start | bytes 6291456 | tf_op jit(solution)/shard_map/all_to_all | solution.py:133
  34.0 31.4 %collective-permute-start.11 = (bf16[96,4,16]{0,2,1:T(8,128)(2,1)S(1)}, bf16[96,4,16]{0,2,1:T(8,128)(2,1)S(1)}, u32[]{:S(2)}, u32[]{:S(2)}) collective-permute-start(bf16[96,4,16]{0,2,1:T(8,128)(2,1)S(1)} %get-tuple-element.168), channel_id=1, source_target_pairs={{1,0},{2,1},{3,2},{5,4},{6,5},{7,6},{9,8},{10,9},{11,10},{13,12},{... | collective-permute-start | bytes 36872 | tf_op jit(solution)/shard_map/ppermute | solution.py:21
  35.3 46.3 %collective-permute-start.10 = (bf16[96,4,16]{0,2,1:T(8,128)(2,1)S(1)}, bf16[96,4,16]{0,2,1:T(8,128)(2,1)S(1)}, u32[]{:S(2)}, u32[]{:S(2)}) collective-permute-start(bf16[96,4,16]{0,2,1:T(8,128)(2,1)S(1)} %get-tuple-element.167), channel_id=1, source_target_pairs={{0,1},{1,2},{2,3},{4,5},{5,6},{6,7},{8,9},{9,10},{10,11},{12,13},{... | collective-permute-start | bytes 36872 | tf_op jit(solution)/shard_map/ppermute | solution.py:19
  99.7 29.8 %all-to-all-start.1 = ((s32[1,32,4,128]{3,2,0,1:T(4,128)}), s32[1,32,4,128]{3,2,0,1:T(4,128)S(1)}, u32[]{:S(2)}, u32[]{:S(2)}) async-start(s32[1,32,4,128]{3,2,0,1:T(4,128)} %bitcast.822), calls=%async_computation.1 | async-start | bytes 131072 | tf_op jit(solution)/shard_map/all_to_all | solution.py:140
  147.9 12.6 %copy-start.9 = (f32[96,610]{1,0:T(8,128)S(1)}, f32[96,610]{1,0:T(8,128)}, u32[]{:S(2)}) copy-start(f32[96,610]{1,0:T(8,128)} %convolution_bitcast_fusion.17) | copy-start | bytes 702724
  147.9 12.6 %copy-start.15 = (f32[96,610]{1,0:T(8,128)S(1)}, f32[96,610]{1,0:T(8,128)}, u32[]{:S(2)}) copy-start(f32[96,610]{1,0:T(8,128)} %convolution_bitcast_fusion.10) | copy-start | bytes 702724
  147.9 12.6 %copy-start.16 = (f32[96,610]{1,0:T(8,128)S(1)}, f32[96,610]{1,0:T(8,128)}, u32[]{:S(2)}) copy-start(f32[96,610]{1,0:T(8,128)} %convolution_bitcast_fusion.11) | copy-start | bytes 702724
  147.9 12.6 %copy-start.17 = (f32[96,610]{1,0:T(8,128)S(1)}, f32[96,610]{1,0:T(8,128)}, u32[]{:S(2)}) copy-start(f32[96,610]{1,0:T(8,128)} %convolution_bitcast_fusion.12) | copy-start | bytes 702724
  149.2 5.3 %collective-permute-start.1 = (bf16[96,1,256]{0,2,1:T(8,128)(2,1)S(1)}, bf16[96,1,256]{0,2,1:T(8,128)(2,1)S(1)}, u32[]{:S(2)}, u32[]{:S(2)}) collective-permute-start(bf16[96,1,256]{0,2,1:T(8,128)(2,1)S(1)} %get-tuple-element.180), channel_id=1, source_target_pairs={{4,0},{8,4},{12,8},{16,12},{20,16},{24,20},{28,24},{5,1},{9,5},{13... | collective-permute-start | bytes 147464 | tf_op jit(solution)/shard_map/ppermute | solution.py:21
  150.5 4.0 collective-permute-start
  154.5 7.6 %collective-permute-start.3 = (bf16[96,4,16]{0,2,1:T(8,128)(2,1)S(1)}, bf16[96,4,16]{0,2,1:T(8,128)(2,1)S(1)}, u32[]{:S(2)}, u32[]{:S(2)}) collective-permute-start(bf16[96,4,16]{0,2,1:T(8,128)(2,1)S(1)} %get-tuple-element.172), channel_id=1, source_target_pairs={{1,0},{2,1},{3,2},{5,4},{6,5},{7,6},{9,8},{10,9},{11,10},{13,12},{... | collective-permute-start | bytes 36872 | tf_op jit(solution)/shard_map/ppermute | solution.py:21
  155.8 6.3 %collective-permute-start.2 = (bf16[96,4,16]{0,2,1:T(8,128)(2,1)S(1)}, bf16[96,4,16]{0,2,1:T(8,128)(2,1)S(1)}, u32[]{:S(2)}, u32[]{:S(2)}) collective-permute-start(bf16[96,4,16]{0,2,1:T(8,128)(2,1)S(1)} %get-tuple-element.171), channel_id=1, source_target_pairs={{0,1},{1,2},{2,3},{4,5},{5,6},{6,7},{8,9},{9,10},{10,11},{12,13},{... | collective-permute-start | bytes 36872 | tf_op jit(solution)/shard_map/ppermute | solution.py:19
  172.4 18.6 %collective-permute-start.5 = (bf16[96,1,256]{0,2,1:T(8,128)(2,1)S(1)}, bf16[96,1,256]{0,2,1:T(8,128)(2,1)S(1)}, u32[]{:S(2)}, u32[]{:S(2)}) collective-permute-start(bf16[96,1,256]{0,2,1:T(8,128)(2,1)S(1)} %get-tuple-element.178), channel_id=1, source_target_pairs={{4,0},{8,4},{12,8},{16,12},{20,16},{24,20},{28,24},{5,1},{9,5},{13... | collective-permute-start | bytes 147464 | tf_op jit(solution)/shard_map/ppermute | solution.py:21
  173.7 17.3 %collective-permute-start.4 = (bf16[96,1,256]{0,2,1:T(8,128)(2,1)S(1)}, bf16[96,1,256]{0,2,1:T(8,128)(2,1)S(1)}, u32[]{:S(2)}, u32[]{:S(2)}) collective-permute-start(bf16[96,1,256]{0,2,1:T(8,128)(2,1)S(1)} %get-tuple-element.177), channel_id=1, source_target_pairs={{0,4},{4,8},{8,12},{12,16},{16,20},{20,24},{24,28},{1,5},{5,9},{9,... | collective-permute-start | bytes 147464 | tf_op jit(solution)/shard_map/ppermute | solution.py:19
  177.7 19.3 %collective-permute-start.13 = (bf16[96,1,256]{0,2,1:T(8,128)(2,1)S(1)}, bf16[96,1,256]{0,2,1:T(8,128)(2,1)S(1)}, u32[]{:S(2)}, u32[]{:S(2)}) collective-permute-start(bf16[96,1,256]{0,2,1:T(8,128)(2,1)S(1)} %get-tuple-element.174), channel_id=1, source_target_pairs={{4,0},{8,4},{12,8},{16,12},{20,16},{24,20},{28,24},{5,1},{9,5},{13... | collective-permute-start | bytes 147464 | tf_op jit(solution)/shard_map/ppermute | solution.py:21
  179.0 18.0 %collective-permute-start.12 = (bf16[96,1,256]{0,2,1:T(8,128)(2,1)S(1)}, bf16[96,1,256]{0,2,1:T(8,128)(2,1)S(1)}, u32[]{:S(2)}, u32[]{:S(2)}) collective-permute-start(bf16[96,1,256]{0,2,1:T(8,128)(2,1)S(1)} %get-tuple-element.173), channel_id=1, source_target_pairs={{0,4},{4,8},{8,12},{12,16},{16,20},{20,24},{24,28},{1,5},{5,9},{9,... | collective-permute-start | bytes 147464 | tf_op jit(solution)/shard_map/ppermute | solution.py:19
  191.1 12.0 %collective-permute-start.7 = (bf16[96,4,16]{0,2,1:T(8,128)(2,1)S(1)}, bf16[96,4,16]{0,2,1:T(8,128)(2,1)S(1)}, u32[]{:S(2)}, u32[]{:S(2)}) collective-permute-start(bf16[96,4,16]{0,2,1:T(8,128)(2,1)S(1)} %get-tuple-element.170), channel_id=1, source_target_pairs={{1,0},{2,1},{3,2},{5,4},{6,5},{7,6},{9,8},{10,9},{11,10},{13,12},{... | collective-permute-start | bytes 36872 | tf_op jit(solution)/shard_map/ppermute | solution.py:21
  192.4 10.7 %collective-permute-start.6 = (bf16[96,4,16]{0,2,1:T(8,128)(2,1)S(1)}, bf16[96,4,16]{0,2,1:T(8,128)(2,1)S(1)}, u32[]{:S(2)}, u32[]{:S(2)}) collective-permute-start(bf16[96,4,16]{0,2,1:T(8,128)(2,1)S(1)} %get-tuple-element.169), channel_id=1, source_target_pairs={{0,1},{1,2},{2,3},{4,5},{5,6},{6,7},{8,9},{9,10},{10,11},{12,13},{... | collective-permute-start | bytes 36872 | tf_op jit(solution)/shard_map/ppermute | solution.py:19
  197.0 13.2 %collective-permute-start.15 = (bf16[96,4,16]{0,2,1:T(8,128)(2,1)S(1)}, bf16[96,4,16]{0,2,1:T(8,128)(2,1)S(1)}, u32[]{:S(2)}, u32[]{:S(2)}) collective-permute-start(bf16[96,4,16]{0,2,1:T(8,128)(2,1)S(1)} %get-tuple-element.166), channel_id=1, source_target_pairs={{1,0},{2,1},{3,2},{5,4},{6,5},{7,6},{9,8},{10,9},{11,10},{13,12},{... | collective-permute-start | bytes 36872 | tf_op jit(solution)/shard_map/ppermute | solution.py:21
  198.3 11.9 %collective-permute-start.14 = (bf16[96,4,16]{0,2,1:T(8,128)(2,1)S(1)}, bf16[96,4,16]{0,2,1:T(8,128)(2,1)S(1)}, u32[]{:S(2)}, u32[]{:S(2)}) collective-permute-start(bf16[96,4,16]{0,2,1:T(8,128)(2,1)S(1)} %get-tuple-element.165), channel_id=1, source_target_pairs={{0,1},{1,2},{2,3},{4,5},{5,6},{6,7},{8,9},{9,10},{10,11},{12,13},{... | collective-permute-start | bytes 36872 | tf_op jit(solution)/shard_map/ppermute | solution.py:19
  246.7 190.1 %all-to-all-start.2 = ((bf16[96,32,4,128]{3,2,0,1:T(4,128)(2,1)}), bf16[96,32,4,128]{3,2,0,1:T(4,128)(2,1)S(1)}, u32[]{:S(2)}, u32[]{:S(2)}) async-start(bf16[96,32,4,128]{3,2,0,1:T(4,128)(2,1)} %copy.59), calls=%async_computation.2 | async-start | bytes 6291456 | tf_op jit(solution)/shard_map/all_to_all | solution.py:198
  253.5 179.9 %all-reduce.13.cloned.1.call-start = ((), (), s32[]{:S(2)}) async-start(), calls=%async_computation.3 | async-start | bytes 5308416 | tf_op jit(solution)/shard_map/psum | solution.py:204
  (24 other events, 106.8 us)
Sparse Core Ops, SparseCore 0:
  278.8 154.5 all-reduce.12
where the time goes:
time: 455 us; the launch traced here: 448 us
  waiting for transfers between devices  180 us (40%)
  matrix products  101 us (22%)
  starting transfers between devices  79 us (17%)
  local copies, waits for them, and re-layouts  55 us (12%)
  between operations  16.2 us (4%)
  other arithmetic  8.65 us (2%)
  loops' own time  7.81 us (2%)
    psum x1, waiting for transfers between devices, on_device(): total_one, total_two = lax.psum((part_one, part_two), ('gx', 'sa'))  139 us
    dot_general x108, matrix products, convolve(): lax.dot_general(weight[offset_k], piece, (((0,), (0,)), ((), ())), prefer...  44.6 us
    ppermute x8, starting transfers between devices, with_halo(): lax.ppermute(tail, axis, [(i, (i + 1) % count) for i in range(ends)])  33.8 us
    dot_general x54, matrix products, weight_grad(): lax.dot_general(piece, grad_span, (((1,), (1,)), ((), ())), preferred_ele...  31 us
    ppermute x8, waiting for transfers between devices, with_halo(): lax.ppermute(head, axis, [((i + 1) % count, i) for i in range(ends)])  21.1 us
    all_to_all x1, starting transfers between devices, on_device(): lax.all_to_all(send_places.reshape(1, devices, capacity, slot_len), ('gx'...  19.9 us
    ppermute x8, waiting for transfers between devices, with_halo(): lax.ppermute(tail, axis, [(i, (i + 1) % count) for i in range(ends)])  16.2 us
    dot_general x2, matrix products, add_block(): jnp.dot(block_feats, one_hot, preferred_element_type=jnp.float32)  10.7 us
  transfers between devices with their start and end apart: 20, of which 4 were waited for; matrix products, arithmetic and copies ran while one was open for 23% of the time, Pallas kernels for 0%

commit v1 on v0

v1 whole, which is shorter than its diff:
```python
import functools
import math

import jax
import jax.numpy as jnp
from jax import lax
from jax.experimental import pallas as pl
from jax.experimental.pallas import tpu as pltpu
from jax.sharding import PartitionSpec as P

EDGE = 16
LANES = 128
BF = jnp.bfloat16
F32 = jnp.float32
MESH = pl.DeviceIdType.MESH
DIRS = [(a, b) for a in (-1, 0, 1) for b in (-1, 0, 1) if (a, b) != (0, 0)]
VMEM_LIMIT = 60 * 1024 * 1024


def bit_orders(gx_count, sa_count):
    gx_bits = [("gx", b) for b in range(gx_count.bit_length() - 1)]
    sa_bits = [("sa", b) for b in range(sa_count.bit_length() - 1)]
    return (
        gx_bits[:1] + gx_bits[1:] + sa_bits,
        gx_bits[:1] + gx_bits[1:][::-1] + sa_bits[::-1],
    )


def bit_of(coord, bit):
    return (coord // (1 << bit)) % 2


def position(order, g, s):
    place = 0
    for axis, bit in order:
        place = place * 2 + bit_of(g if axis == "gx" else s, bit)
    return place


def one_hot(places_row, cell_total):
    cells = lax.broadcasted_iota(jnp.int32, (cell_total, places_row.shape[1]), 0)
    return jnp.where(cells == places_row, 1.0, 0.0).astype(BF)


def scatter_kernel(place0, place1, feats, places, dense, total):
    rows = feats.shape[0]
    owners = dense.shape[1]

    def clear(i, carry):
        total[:, i] = jnp.zeros(total.shape[:1] + total.shape[2:], F32)
        return carry

    lax.fori_loop(0, owners, clear, 0)

    def add_row(r, carry):
        hot = one_hot(places[r], 4 * LANES)
        part = lax.dot_general(feats[r], hot, (((1,), (1,)), ((), ())), preferred_element_type=F32)
        at0 = place0[r]
        at1 = place1[r]
        for b in range(2):
            total[0, at0, b] += part[:, b * LANES : (b + 1) * LANES]
            total[1, at1, b] += part[:, (b + 2) * LANES : (b + 3) * LANES]
        return carry

    lax.fori_loop(0, rows, add_row, 0)

    def store(i, carry):
        dense[:, i] = total[:, i].astype(BF)
        return carry

    lax.fori_loop(0, owners, store, 0)


def gather_kernel(place0, place1, cells, places, out):
    rows = out.shape[0]

    def one_row(r, carry):
        hot = one_hot(places[r], 4 * LANES)
        at0 = place0[r]
        at1 = place1[r]
        full = jnp.concatenate(
            [cells[0, at0, 0], cells[0, at0, 1], cells[1, at1, 0], cells[1, at1, 1]], axis=1
        )
        out[r] = jnp.dot(full, hot, preferred_element_type=F32).astype(BF)
        return carry

    lax.fori_loop(0, rows, one_row, 0)


def main_kernel(
    gx_count, sa_count, factor,
    dense, occ, cot, w1f, w2f, w1b, w2b,
    out_field, cells_out, gw1, gw2,
    ev, eh, eg, ef, sv, sh, sg, pre, gh,
    acc, stage, recv, cells_buf, wacc, wstage, wrecv, wall,
    local_sem, own_sem, halo_send, halo_recv, rs_send, rs_recv, ag_send, ag_recv,
    ws_send, ws_recv, wg_send, wg_recv,
):
    g = lax.axis_index("gx")
    s = lax.axis_index("sa")
    orders = bit_orders(gx_count, sa_count)
    steps = len(orders[0])
    devices = gx_count * sa_count
    channels = cot.shape[0]
    wide = 9 * channels

    for e in (ev, eh, eg, ef):
        e[...] = jnp.zeros(e.shape, BF)
    real_rows = 27 * channels
    pad_rows = wacc.shape[1] - real_rows
    if pad_rows:
        for c in range(2):
            wacc[c, real_rows:] = jnp.zeros((pad_rows, channels), F32)

    def partner(axis, bit):
        coord = g if axis == "gx" else s
        other = coord + (1 << bit) * (1 - 2 * bit_of(coord, bit))
        return (other, s) if axis == "gx" else (g, other)

    def inside(dg, ds):
        gg = g + dg
        ss = s + ds
        return (gg >= 0) & (gg < gx_count) & (ss >= 0) & (ss < sa_count)

    barrier = pltpu.get_barrier_semaphore()
    expected = jnp.int32(steps)
    for axis, bit in orders[0]:
        pl.semaphore_signal(barrier, inc=1, device_id=partner(axis, bit), device_id_type=MESH)
    for dg, ds in DIRS:
        expected = expected + inside(dg, ds).astype(jnp.int32)

        @pl.when(inside(dg, ds))
        def _():
            pl.semaphore_signal(barrier, inc=1, device_id=(g + dg, s + ds), device_id_type=MESH)

    pl.semaphore_wait(barrier, expected)

    def halo_copy(e, field, d):
        dg, ds = DIRS[d]
        px, dx = {-1: (pl.ds(1, 1), pl.ds(3, 1)), 0: (pl.ds(1, 2), pl.ds(1, 2)),
                  1: (pl.ds(2, 1), pl.ds(0, 1))}[dg]
        py, dy = {-1: (pl.ds(1, 1), pl.ds(3, 1)), 0: (pl.ds(1, 2), pl.ds(1, 2)),
                  1: (pl.ds(2, 1), pl.ds(0, 1))}[ds]
        return pltpu.make_async_remote_copy(
            src_ref=e.at[px, py], dst_ref=e.at[dx, dy],
            send_sem=halo_send.at[field, d], recv_sem=halo_recv.at[field, d],
            device_id=(g + dg, s + ds), device_id_type=MESH,
        )

    def halo_start(e, field):
        for d, (dg, ds) in enumerate(DIRS):
            @pl.when(inside(dg, ds))
            def _():
                halo_copy(e, field, d).start()

    def halo_wait_recv(e, field):
        for d, (dg, ds) in enumerate(DIRS):
            @pl.when(inside(-dg, -ds))
            def _():
                halo_copy(e, field, d).wait_recv()

    def halo_wait_send(e, field):
        for d, (dg, ds) in enumerate(DIRS):
            @pl.when(inside(dg, ds))
            def _():
                halo_copy(e, field, d).wait_send()

    def my_bit(order, t):
        axis, bit = order[t]
        return bit_of(g if axis == "gx" else s, bit)

    half = devices // 2
    offs = [0]
    for t in range(steps):
        offs.append(offs[-1] + (devices >> (t + 1)))

    def rs_copy(st, t):
        n = devices >> (t + 1)
        if t == 0:
            src = dense.at[st, pl.ds((1 - my_bit(orders[st], 0)) * half, half)]
        else:
            src = stage.at[st, pl.ds(offs[t] - half, n)]
        return pltpu.make_async_remote_copy(
            src_ref=src, dst_ref=recv.at[st, pl.ds(offs[t], n)],
            send_sem=rs_send.at[st, t], recv_sem=rs_recv.at[st, t],
            device_id=partner(*orders[st][t]), device_id_type=MESH,
        )

    def local_copy(st):
        return pltpu.make_async_copy(
            dense.at[st, pl.ds(my_bit(orders[st], 0) * half, half)], stage.at[st], local_sem.at[st]
        )

    for st in range(2):
        rs_copy(st, 0).start()
        local_copy(st).start()

    def write_interior(e, value):
        for p in range(2):
            for b in range(2):
                lo = (2 * p + b) * LANES
                e[p + 1, b + 1] = value[:, lo : lo + LANES]

    def read_interior(e):
        return jnp.concatenate([e[1, 1], e[1, 2], e[2, 1], e[2, 2]], axis=1)

    def build(e, sref):
        z = lax.broadcasted_iota(jnp.int32, (channels, 4 * LANES), 1) % EDGE
        for p in range(4):
            full = jnp.concatenate([e[p, b] for b in range(4)], axis=1).astype(F32)
            for dz in (-1, 0, 1):
                if dz == 1:
                    src = jnp.where(z == 0, 0.0, full)
                elif dz == -1:
                    src = jnp.where(z == EDGE - 1, 0.0, full)
                else:
                    src = full
                for dy in (-1, 0, 1):
                    shift = EDGE * dy + dz
                    turned = src if shift == 0 else pltpu.roll(src, (-shift) % (4 * LANES), 1)
                    k = (dy + 1) * 3 + dz + 1
                    sref[k * channels : (k + 1) * channels, 2 * p * LANES : 2 * (p + 1) * LANES] = (
                        turned[:, LANES : 3 * LANES].astype(BF)
                    )

    def conv(w, sref):
        total = None
        for dx in range(3):
            term = jnp.dot(
                w[dx], sref[:, 2 * dx * LANES : (2 * dx + 4) * LANES], preferred_element_type=F32
            )
            total = term if total is None else total + term
        return total

    def weight_part(c, sref, value):
        for dx in range(3):
            wacc[c, dx * wide : (dx + 1) * wide] = lax.dot_general(
                sref[:, 2 * dx * LANES : (2 * dx + 4) * LANES], value,
                (((1,), (1,)), ((), ())), preferred_element_type=F32,
            )

    live = occ[...]
    write_interior(eg, (live * cot[...].astype(F32)).astype(BF))
    halo_start(eg, 2)
    halo_wait_recv(eg, 2)
    build(eg, sg)
    gh[...] = conv(w2b, sg)

    for st in range(2):
        local_copy(st).wait()
    bases = [0, 0]
    for t in range(steps):
        n = devices >> (t + 1)
        for st in range(2):
            rs_copy(st, t).wait_recv()
            if t == 0:
                def fold(i, carry, st=st):
                    acc[st, i] = stage[st, i].astype(F32) + recv[st, i].astype(F32)
                    return carry
            else:
                bases[st] = bases[st] + my_bit(orders[st], t) * n

                def fold(i, carry, st=st, base=bases[st], off=offs[t]):
                    acc[st, base + i] = acc[st, base + i] + recv[st, off + i].astype(F32)
                    return carry
            lax.fori_loop(0, n, fold, 0)
            if t + 1 < steps:
                m = n // 2
                give = bases[st] + (1 - my_bit(orders[st], t + 1)) * m

                def put(i, carry, st=st, give=give, off=offs[t + 1] - half):
                    stage[st, off + i] = acc[st, give + i].astype(BF)
                    return carry
                lax.fori_loop(0, m, put, 0)
                rs_copy(st, t + 1).start()
    for st in range(2):
        for b in range(2):
            lo = (2 * st + b) * LANES
            ev[st + 1, b + 1] = (live[:, lo : lo + LANES] * acc[st, bases[st], b]).astype(BF)
    halo_start(ev, 0)
    halo_wait_recv(ev, 0)
    build(ev, sv)
    pre[...] = conv(w1f, sv)
    first = pre[...]
    sig = 1.0 / (1.0 + jnp.exp(-first))
    write_interior(eh, (live * first * sig).astype(BF))
    halo_start(eh, 1)
    write_interior(ef, (live * gh[...] * (sig * (1.0 + first * (1.0 - sig)))).astype(BF))
    halo_start(ef, 3)
    weight_part(0, sv, read_interior(ef))
    halo_wait_recv(eh, 1)
    build(eh, sh)
    weight_part(1, sh, read_interior(eg))
    rb = wacc.shape[1] // devices

    def ws_copy(c, t):
        n = (devices >> (t + 1)) * rb
        return pltpu.make_async_remote_copy(
            src_ref=wstage.at[c, pl.ds(offs[t] * rb, n)], dst_ref=wrecv.at[c, pl.ds(offs[t] * rb, n)],
            send_sem=ws_send.at[c, t], recv_sem=ws_recv.at[c, t],
            device_id=partner(*orders[c][t]), device_id_type=MESH,
        )

    wbase = [0, 0]

    def ws_begin(c, t):
        m = devices >> (t + 1)
        give = wbase[c] + (1 - my_bit(orders[c], t)) * m

        def put(i, carry):
            wstage[c, pl.ds(pl.multiple_of((offs[t] + i) * rb, 16), rb)] = wacc[
                c, pl.ds(pl.multiple_of((give + i) * rb, 16), rb)].astype(BF)
            return carry
        lax.fori_loop(0, m, put, 0)
        ws_copy(c, t).start()

    def ws_finish(c, t):
        m = devices >> (t + 1)
        wbase[c] = wbase[c] + my_bit(orders[c], t) * m
        ws_copy(c, t).wait_recv()
        base = wbase[c]

        def fold(i, carry):
            at = pl.ds(pl.multiple_of((base + i) * rb, 16), rb)
            wacc[c, at] = wacc[c, at] + wrecv[
                c, pl.ds(pl.multiple_of((offs[t] + i) * rb, 16), rb)].astype(F32)
            return carry
        lax.fori_loop(0, m, fold, 0)

    for c in range(2):
        ws_begin(c, 0)
    halo_wait_recv(ef, 3)
    build(ef, sg)
    cells = (live * conv(w1b, sg)).astype(BF)
    spots = [position(orders[st], g, s) for st in range(2)]

    def own_copy(st):
        return pltpu.make_async_copy(
            cells_buf.at[st], cells_out.at[st, spots[st]], own_sem.at[st]
        )

    for st in range(2):
        for b in range(2):
            lo = (2 * st + b) * LANES
            cells_buf[st, b] = cells[:, lo : lo + LANES]
        own_copy(st).start()

    def ag_copy(st, t):
        n = 1 << t
        held = cells_out.at[st, pl.ds((spots[st] // n) * n, n)]
        return pltpu.make_async_remote_copy(
            src_ref=held, dst_ref=held,
            send_sem=ag_send.at[st, t], recv_sem=ag_recv.at[st, t],
            device_id=partner(*orders[st][steps - 1 - t]), device_id_type=MESH,
        )

    def ag_wait_recv(st, t):
        n = 1 << t
        mine = spots[st] // n
        theirs = mine + 1 - 2 * (mine % 2)
        there = cells_out.at[st, pl.ds(theirs * n, n)]
        pltpu.make_async_remote_copy(
            src_ref=there, dst_ref=there,
            send_sem=ag_send.at[st, t], recv_sem=ag_recv.at[st, t],
            device_id=partner(*orders[st][steps - 1 - t]), device_id_type=MESH,
        ).wait_recv()

    for st in range(2):
        own_copy(st).wait()
        ag_copy(st, 0).start()
    out_field[...] = (live * conv(w2f, sh)).astype(BF)
    for t in range(steps):
        for st in range(2):
            ag_wait_recv(st, t)
            if t + 1 < steps:
                ag_copy(st, t + 1).start()
        for c in range(2):
            ws_finish(c, t)
            if t + 1 < steps:
                ws_begin(c, t + 1)

    def wg_ref(c, block, n):
        return wall.at[c, pl.ds(pl.multiple_of(block * rb, 16), n * rb)]

    def wg_copy(c, t):
        n = 1 << t
        held = wg_ref(c, (spots[c] // n) * n, n)
        return pltpu.make_async_remote_copy(
            src_ref=held, dst_ref=held,
            send_sem=wg_send.at[c, t], recv_sem=wg_recv.at[c, t],
            device_id=partner(*orders[c][steps - 1 - t]), device_id_type=MESH,
        )

    for c in range(2):
        at = pl.ds(pl.multiple_of(spots[c] * rb, 16), rb)
        wall[c, at] = (wacc[c, at] * factor).astype(BF)
        wg_copy(c, 0).start()
    for t in range(steps):
        n = 1 << t
        for c in range(2):
            mine = spots[c] // n
            there = wg_ref(c, (mine + 1 - 2 * (mine % 2)) * n, n)
            pltpu.make_async_remote_copy(
                src_ref=there, dst_ref=there,
                send_sem=wg_send.at[c, t], recv_sem=wg_recv.at[c, t],
                device_id=partner(*orders[c][steps - 1 - t]), device_id_type=MESH,
            ).wait_recv()
            if t + 1 < steps:
                wg_copy(c, t + 1).start()
    gw1[...] = wall[0, :real_rows].astype(F32)
    gw2[...] = wall[1, :real_rows].astype(F32)

    for st in range(2):
        for t in range(steps):
            rs_copy(st, t).wait_send()
            ag_copy(st, t).wait_send()
            ws_copy(st, t).wait_send()
            wg_copy(st, t).wait_send()
    for field, e in enumerate((ev, eh, eg, ef)):
        halo_wait_send(e, field)


def on_device(
    gx_count, sa_count,
    scan_feats, row_owner, row_voxels, row_count, occupancy, weight_one, weight_two, cotangent,
):
    channels, row_total, slot_len = scan_feats.shape
    slab_len, plane_len = occupancy.shape
    cell_total = slab_len * plane_len
    devices = gx_count * sa_count
    orders = bit_orders(gx_count, sa_count)
    steps = len(orders[0])
    owner_g = row_owner // sa_count
    owner_s = row_owner % sa_count
    place0 = position(orders[0], owner_g, owner_s)
    place1 = position(orders[1], owner_g, owner_s)
    is_live = jnp.arange(slot_len)[None, :] < row_count[:, None]
    places = jnp.where(is_live, row_voxels, -1).reshape(row_total, 1, slot_len)
    feats = jnp.transpose(scan_feats, (1, 0, 2))
    vmem = pl.BlockSpec(memory_space=pltpu.VMEM)
    smem = pl.BlockSpec(memory_space=pltpu.SMEM)
    hbm = pl.BlockSpec(memory_space=pl.ANY)
    grid_shape = (2, devices, 2, channels, LANES)
    dense = pl.pallas_call(
        scatter_kernel,
        out_shape=jax.ShapeDtypeStruct(grid_shape, BF),
        in_specs=[smem, smem, vmem, vmem],
        out_specs=vmem,
        scratch_shapes=[pltpu.VMEM(grid_shape, F32)],
        compiler_params=pltpu.CompilerParams(vmem_limit_bytes=VMEM_LIMIT),
        name="scatter_rows",
    )(place0, place1, feats, places)

    def forward(weight):
        return jnp.transpose(weight.reshape(3, 9 * channels, channels), (0, 2, 1))

    def backward(weight):
        back = weight[::-1].reshape(3, 9, channels, channels)
        return jnp.transpose(back, (0, 2, 1, 3)).reshape(3, channels, 9 * channels)

    real_rows = 27 * channels
    rb = -(-real_rows // (devices * 16)) * 16
    wrows = rb * devices
    half = devices // 2
    block = (2, channels, LANES)
    field = pltpu.VMEM((4, 4, channels, LANES), BF)
    stacked = pltpu.VMEM((9 * channels, 8 * LANES), BF)
    plane = pltpu.VMEM((channels, cell_total), F32)
    dma = pltpu.SemaphoreType.DMA
    factor = 1.0 / math.sqrt(cell_total * devices)
    out_field, cells, gw1, gw2 = pl.pallas_call(
        functools.partial(main_kernel, gx_count, sa_count, factor),
        out_shape=(
            jax.ShapeDtypeStruct((channels, cell_total), BF),
            jax.ShapeDtypeStruct(grid_shape, BF),
            jax.ShapeDtypeStruct((real_rows, channels), F32),
            jax.ShapeDtypeStruct((real_rows, channels), F32),
        ),
        in_specs=[hbm] + [vmem] * 6,
        out_specs=(vmem, hbm, vmem, vmem),
        scratch_shapes=[
            field, field, field, field, stacked, stacked, stacked, plane, plane,
            pltpu.VMEM((2, half) + block, F32),
            pltpu.VMEM((2, half) + block, BF),
            pltpu.VMEM((2, devices) + block, BF),
            pltpu.VMEM((2,) + block, BF),
            pltpu.VMEM((2, wrows, channels), F32),
            pltpu.VMEM((2, wrows, channels), BF),
            pltpu.VMEM((2, wrows, channels), BF),
            pltpu.VMEM((2, wrows, channels), BF),
            dma((2,)), dma((2,)), dma((4, 8)), dma((4, 8)),
            dma((2, steps)), dma((2, steps)), dma((2, steps)), dma((2, steps)),
            dma((2, steps)), dma((2, steps)), dma((2, steps)), dma((2, steps)),
        ],
        compiler_params=pltpu.CompilerParams(
            collective_id=0, has_side_effects=True, vmem_limit_bytes=VMEM_LIMIT
        ),
        name="conv_pair",
    )(
        dense,
        occupancy.astype(F32).reshape(1, cell_total),
        cotangent.reshape(channels, cell_total),
        forward(weight_one), forward(weight_two), backward(weight_one), backward(weight_two),
    )
    rows_out = pl.pallas_call(
        gather_kernel,
        out_shape=jax.ShapeDtypeStruct((row_total, channels, slot_len), BF),
        in_specs=[smem, smem, vmem, vmem],
        out_specs=vmem,
        compiler_params=pltpu.CompilerParams(vmem_limit_bytes=VMEM_LIMIT),
        name="gather_rows",
    )(place0, place1, cells, places)
    grad_scan = jnp.transpose(rows_out, (1, 0, 2))
    weights = (27, channels, channels)
    return (
        out_field.reshape(channels, slab_len, plane_len),
        grad_scan,
        gw1.reshape(weights),
        gw2.reshape(weights),
    )


def solution(mesh):
    return jax.shard_map(
        functools.partial(on_device, mesh.shape["gx"], mesh.shape["sa"]),
        mesh=mesh,
        in_specs=(
            P(None, ("gx", "sa"), None),
            P(("gx", "sa")),
            P(("gx", "sa"), None),
            P(("gx", "sa")),
            P("gx", "sa"),
            P(),
            P(),
            P(None, "gx", "sa"),
        ),
        out_specs=(P(None, "gx", "sa"), P(None, ("gx", "sa"), None), P(), P()),
        check_vma=False,
    )
```

time: 455 us -> 158 us (0.35); the launches traced: 448 us -> 157 us
  waiting for transfers between devices: 180 us -> 0 us
  Pallas kernels: 0 us -> 134 us
  matrix products: 101 us -> 0 us
  starting transfers between devices: 79 us -> 0 us
  local copies, waits for them, and re-layouts: 55 us -> 18.1 us
  between operations: 16.2 us -> 0.68 us
  loops' own time: 7.81 us -> 0 us
  other arithmetic: 8.65 us -> 4.01 us
    psum x1 -> x0, waiting for transfers between devices: 139 us -> none  [on_device(): total_one, total_two = lax.psum((part_one, part_two), ('gx', 'sa'))]
    pallas_call x0 -> x3, Pallas kernels: none -> 134 us  [the longest x1 103 us: on_device(): pl.pallas_call(functools.partial(main_kernel, gx_count, sa_count, factor)...]
    dot_general x169 -> x0, matrix products: 101 us -> none  [the longest x108 44.6 us: convolve(): lax.dot_general(weight[offset_k], piece, (((0,), (0,)), ((), ())), prefer...]
    ppermute x16 -> x0, starting transfers between devices: 44.2 us -> none  [the longest x8 33.8 us: with_halo(): lax.ppermute(tail, axis, [(i, (i + 1) % count) for i in range(ends)])]
    ppermute x16 -> x0, waiting for transfers between devices: 37.2 us -> none  [the longest x8 21.1 us: with_halo(): lax.ppermute(head, axis, [((i + 1) % count, i) for i in range(ends)])]
    all_to_all x3 -> x0, starting transfers between devices: 34.5 us -> none  [the longest x1 19.9 us: on_device(): lax.all_to_all(send_places.reshape(1, devices, capacity, slot_len), ('gx'...]
    reshape x14 -> x7, local copies, waits for them, and re-layouts: 23.1 us -> 7.59 us  [the longest x2 3.2 us: forward(): return jnp.transpose(weight.reshape(3, 9 * channels, channels), (0, 2, 1))]
    transpose x3 -> x0, local copies, waits for them, and re-layouts: 8.02 us -> none  [the longest x1 5.15 us: on_device(): jnp.moveaxis(picked_blocks, 1, 0)]
  transfers between devices with their start and end apart: 20 -> 0, of which waited for: 4 -> 0; matrix products, arithmetic and copies ran while one was open for 23% -> 0% of each run, Pallas kernels for 0% -> 0%
where the time goes in v1:
time: 158 us; the launch traced here: 157 us
  Pallas kernels  134 us (85%)
  local copies, waits for them, and re-layouts  18.1 us (11%)
  other arithmetic  4.01 us (3%)
    pallas_call x1, Pallas kernels, on_device(): pl.pallas_call(functools.partial(main_kernel, gx_count, sa_count, factor)...  103 us
    pallas_call x1, Pallas kernels, on_device(): pl.pallas_call(scatter_kernel, out_shape=jax.ShapeDtypeStruct(grid_shape,...  16.9 us
    pallas_call x1, Pallas kernels, on_device(): pl.pallas_call(gather_kernel, out_shape=jax.ShapeDtypeStruct((row_total,...  14.1 us
    unnamed x16, local copies, waits for them, and re-layouts  10.4 us
    reshape x2, local copies, waits for them, and re-layouts, forward(): return jnp.transpose(weight.reshape(3, 9 * channels, channels), (0, 2, 1))  3.2 us

profile of v1, /device:TPU:0, one launch (start us, length us, event | category | flops | bytes accessed | tf_op | source)
XLA Modules:
  0.0 157.0 jit_solution(10632689550410709773)
XLA Ops:
  0.6 0.8 convert_bitcast_fusion
  1.4 0.5 copy.24
  1.9 1.2 multiply_add_fusion
  3.1 0.6 multiply_add_fusion.1.place0
  3.7 1.4 fusion
  5.2 1.5 copy.25
  6.7 2.1 %copy.18 = bf16[3,864,96]{1,2,0:T(8,128)(2,1)} copy(bf16[3,864,96]{2,1,0:T(8,128)(2,1)} %bitcast.28) | data formatting | bytes 995328 | tf_op jit(solution)/shard_map/reshape | solution.py:455
  8.9 1.1 copy.17
  10.0 0.0 copy-start.1
  10.0 0.3 copy.19
  10.3 1.1 copy.21.w1b
  11.5 0.0 copy-start.2
  11.5 0.3 copy.20
  11.8 1.1 copy.22.w2b
  12.9 0.0 copy-done.2
  12.9 2.2 %copy.27 = bf16[96,64,128]{2,0,1:T(8,128)(2,1)} copy(bf16[96,64,128]{2,1,0:T(8,128)(2,1)S(1)} %copy-done.2) | data formatting | bytes 3145728 | tf_op args[0]
  15.1 16.9 %scatter_rows.1.dense = bf16[2,32,2,96,128]{4,3,2,1,0:T(8,128)(2,1)} custom-call(s32[64]{0:T(128)} %multiply_add_fusion.1.place0, s32[64]{0:T(128)} %get-tuple-element.20.place1, bf16[64,96,128]{2,1,0:T(8,128)(2,1)} %bitcast.26, s32[64,1,128]{2,1,0:T(1,128)} %bitcast.38), custom_call_target="tpu_custom_call" | custom-call | tf_op jit(solution)/shard_map/scatter_rows/pallas_call | solution.py:444
  32.0 103.3 %conv_pair.1 = (bf16[96,512]{1,0:T(8,128)(2,1)}, bf16[2,32,2,96,128]{4,3,2,1,0:T(8,128)(2,1)}, f32[2592,96]{1,0:T(8,128)}, f32[2592,96]{1,0:T(8,128)}) custom-call(bf16[2,32,2,96,128]{4,3,2,1,0:T(8,128)(2,1)} %scatter_rows.1.dense, f32[1,512]{1,0:T(1,128)} %bitcast.41, bf16[96,512]{1,0:T(8,128)(2,1)} %bitcast.37, bf16[3,96,864]{2,1,0:T(8,128)(2,1)} %bitcast.34, ...), custom_call_target="tpu_custom_call" | custom-call | tf_op jit(solution)/shard_map/conv_pair/pallas_call | solution.py:471
  135.2 1.6 reshape.54
  136.8 14.1 %gather_rows.1 = bf16[64,96,128]{2,1,0:T(8,128)(2,1)} custom-call(s32[64]{0:T(128)} %multiply_add_fusion.1.place0, s32[64]{0:T(128)} %get-tuple-element.20.place1, bf16[2,32,2,96,128]{4,3,2,1,0:T(8,128)(2,1)} %get-tuple-element.9.cells, s32[64,1,128]{2,1,0:T(1,128)} %bitcast.39), custom_call_target="tpu_custom_call" | custom-call | tf_op jit(solution)/shard_map/gather_rows/pallas_call | solution.py:505
  150.9 3.3 %copy.23 = bf16[96,64,128]{2,1,0:T(8,128)(2,1)} copy(bf16[96,64,128]{2,0,1:T(8,128)(2,1)} %bitcast.25) | data formatting | bytes 3145728
  154.2 1.1 copy.30
  155.2 0.7 copy-done.3
  156.0 1.1 copy.31
  (8 shorter events, 0.1 us)
Async XLA Ops:
  0.6 8.2 %copy-start = (bf16[27,96,96]{2,1,0:T(8,128)(2,1)S(1)}, bf16[27,96,96]{2,1,0:T(8,128)(2,1)}, u32[]{:S(2)}) copy-start(bf16[27,96,96]{2,1,0:T(8,128)(2,1)} %param.13) | copy-start | bytes 1492996
  10.0 1.5 copy-start.1
  11.5 1.4 copy-start.2
  150.9 3.3 %copy-start.4 = (f32[2592,96]{1,0:T(8,128)S(1)}, f32[2592,96]{1,0:T(8,128)}, u32[]{:S(2)}) copy-start(f32[2592,96]{1,0:T(8,128)} %get-tuple-element.10) | copy-start | bytes 2985988
  154.2 1.8 %copy-start.3 = (f32[2592,96]{1,0:T(8,128)S(1)}, f32[2592,96]{1,0:T(8,128)}, u32[]{:S(2)}) copy-start(f32[2592,96]{1,0:T(8,128)} %get-tuple-element.11) | copy-start | bytes 2985988

commit v2 on v1

--- a/solution.py
+++ b/solution.py
@@ -14,15 +14,17 @@
 F32 = jnp.float32
 MESH = pl.DeviceIdType.MESH
 DIRS = [(a, b) for a in (-1, 0, 1) for b in (-1, 0, 1) if (a, b) != (0, 0)]
-VMEM_LIMIT = 60 * 1024 * 1024
+VMEM_LIMIT = 62 * 1024 * 1024
 
 
 def bit_orders(gx_count, sa_count):
     gx_bits = [("gx", b) for b in range(gx_count.bit_length() - 1)]
     sa_bits = [("sa", b) for b in range(sa_count.bit_length() - 1)]
+    first, mid = gx_bits[:1], gx_bits[1:]
     return (
-        gx_bits[:1] + gx_bits[1:] + sa_bits,
-        gx_bits[:1] + gx_bits[1:][::-1] + sa_bits[::-1],
+        first + mid + sa_bits,
+        first + mid[1:] + sa_bits[:1] + mid[:1] + sa_bits[1:],
+        first + sa_bits[:1] + mid + sa_bits[1:],
     )
 
 
@@ -37,14 +39,22 @@
     return place
 
 
-def one_hot(places_row, cell_total):
-    cells = lax.broadcasted_iota(jnp.int32, (cell_total, places_row.shape[1]), 0)
-    return jnp.where(cells == places_row, 1.0, 0.0).astype(BF)
-
-
-def scatter_kernel(place0, place1, feats, places, dense, total):
-    rows = feats.shape[0]
+def one_hot(places_pair):
+    both = places_pair.astype(F32).astype(BF)
+    cells = lax.broadcasted_iota(jnp.int32, (2 * LANES, both.shape[1]), 0)
+    cells = cells.astype(F32).astype(BF)
+    one = jnp.ones((), BF)
+    zero = jnp.zeros((), BF)
+    return jnp.concatenate(
+        [jnp.where(cells == both[p : p + 1], one, zero) for p in range(2)], axis=0
+    )
+
+
+def scatter_kernel(spot, feats, places, dense, total):
+    rows, channels, _ = feats.shape
     owners = dense.shape[1]
+    third = channels // 3
+    group = 4
 
     def clear(i, carry):
         total[:, i] = jnp.zeros(total.shape[:1] + total.shape[2:], F32)
@@ -52,17 +62,27 @@
 
     lax.fori_loop(0, owners, clear, 0)
 
-    def add_row(r, carry):
-        hot = one_hot(places[r], 4 * LANES)
-        part = lax.dot_general(feats[r], hot, (((1,), (1,)), ((), ())), preferred_element_type=F32)
-        at0 = place0[r]
-        at1 = place1[r]
-        for b in range(2):
-            total[0, at0, b] += part[:, b * LANES : (b + 1) * LANES]
-            total[1, at1, b] += part[:, (b + 2) * LANES : (b + 3) * LANES]
+    def add_rows(q, carry):
+        parts = []
+        for u in range(group):
+            r = q * group + u
+            parts.append(
+                lax.dot_general(
+                    feats[r], one_hot(places[r]), (((1,), (1,)), ((), ())),
+                    preferred_element_type=F32,
+                )
+            )
+        for u in range(group):
+            r = q * group + u
+            for st in range(3):
+                at = spot[st, r]
+                for b in range(4):
+                    total[st, at, b] += parts[u][
+                        st * third : (st + 1) * third, b * LANES : (b + 1) * LANES
+                    ]
         return carry
 
-    lax.fori_loop(0, rows, add_row, 0)
+    lax.fori_loop(0, rows // group, add_rows, 0)
 
     def store(i, carry):
         dense[:, i] = total[:, i].astype(BF)
@@ -71,29 +91,13 @@
     lax.fori_loop(0, owners, store, 0)
 
 
-def gather_kernel(place0, place1, cells, places, out):
-    rows = out.shape[0]
-
-    def one_row(r, carry):
-        hot = one_hot(places[r], 4 * LANES)
-        at0 = place0[r]
-        at1 = place1[r]
-        full = jnp.concatenate(
-            [cells[0, at0, 0], cells[0, at0, 1], cells[1, at1, 0], cells[1, at1, 1]], axis=1
-        )
-        out[r] = jnp.dot(full, hot, preferred_element_type=F32).astype(BF)
-        return carry
-
-    lax.fori_loop(0, rows, one_row, 0)
-
-
 def main_kernel(
     gx_count, sa_count, factor,
-    dense, occ, cot, w1f, w2f, w1b, w2b,
-    out_field, cells_out, gw1, gw2,
-    ev, eh, eg, ef, sv, sh, sg, pre, gh,
-    acc, stage, recv, cells_buf, wacc, wstage, wrecv, wall,
-    local_sem, own_sem, halo_send, halo_recv, rs_send, rs_recv, ag_send, ag_recv,
+    spot, dense, occ, cot, w1, w2, places,
+    out_field, cells_out, rows_out, wall,
+    ev, eh, eg, ef, sv, sh, sg, pre, gh, w1b, w2b,
+    acc, stage, recv, recv32, cells_buf, wacc, wstage, wrecv, wrecv32,
+    local_sem, own_sem, fetch_sem, halo_send, halo_recv, rs_send, rs_recv, ag_send, ag_recv,
     ws_send, ws_recv, wg_send, wg_recv,
 ):
     g = lax.axis_index("gx")
@@ -106,10 +110,11 @@
 
     for e in (ev, eh, eg, ef):
         e[...] = jnp.zeros(e.shape, BF)
-    real_rows = 27 * channels
+    third = channels // 3
+    real_rows = 2 * wide
     pad_rows = wacc.shape[1] - real_rows
     if pad_rows:
-        for c in range(2):
+        for c in range(3):
             wacc[c, real_rows:] = jnp.zeros((pad_rows, channels), F32)
 
     def partner(axis, bit):
@@ -174,14 +179,26 @@
     for t in range(steps):
         offs.append(offs[-1] + (devices >> (t + 1)))
 
+    def rs_base(st, t):
+        base = 0
+        for u in range(1, t):
+            base = base + my_bit(orders[st], u) * (devices >> (u + 1))
+        return base
+
     def rs_copy(st, t):
         n = devices >> (t + 1)
         if t == 0:
             src = dense.at[st, pl.ds((1 - my_bit(orders[st], 0)) * half, half)]
+        elif t < 2:
+            src = stage.at[st, pl.ds(offs[t] - half, n)]
         else:
-            src = stage.at[st, pl.ds(offs[t] - half, n)]
+            src = acc.at[st, pl.ds(rs_base(st, t) + (1 - my_bit(orders[st], t)) * n, n)]
+        if t < 2:
+            dst = recv.at[st, pl.ds(offs[t], n)]
+        else:
+            dst = recv32.at[st, pl.ds(offs[t] - offs[2], n)]
         return pltpu.make_async_remote_copy(
-            src_ref=src, dst_ref=recv.at[st, pl.ds(offs[t], n)],
+            src_ref=src, dst_ref=dst,
             send_sem=rs_send.at[st, t], recv_sem=rs_recv.at[st, t],
             device_id=partner(*orders[st][t]), device_id_type=MESH,
         )
@@ -191,7 +208,7 @@
             dense.at[st, pl.ds(my_bit(orders[st], 0) * half, half)], stage.at[st], local_sem.at[st]
         )
 
-    for st in range(2):
+    for st in range(3):
         rs_copy(st, 0).start()
         local_copy(st).start()
 
@@ -226,15 +243,30 @@
     def conv(w, sref):
         total = None
         for dx in range(3):
+            term = lax.dot_general(
+                w[9 * dx : 9 * dx + 9].reshape(wide, channels),
+                sref[:, 2 * dx * LANES : (2 * dx + 4) * LANES],
+                (((0,), (0,)), ((), ())), preferred_element_type=F32,
+            )
+            total = term if total is None else total + term
+        return total
+
+    def conv_back(w, sref):
+        total = None
+        for dx in range(3):
             term = jnp.dot(
                 w[dx], sref[:, 2 * dx * LANES : (2 * dx + 4) * LANES], preferred_element_type=F32
             )
             total = term if total is None else total + term
         return total
 
+    for w, back in ((w2, w2b), (w1, w1b)):
+        for k in range(27):
+            back[k // 9, :, (k % 9) * channels : (k % 9 + 1) * channels] = w[26 - k]
+
     def weight_part(c, sref, value):
         for dx in range(3):
-            wacc[c, dx * wide : (dx + 1) * wide] = lax.dot_general(
+            wacc[dx, c * wide : (c + 1) * wide] = lax.dot_general(
                 sref[:, 2 * dx * LANES : (2 * dx + 4) * LANES], value,
                 (((1,), (1,)), ((), ())), preferred_element_type=F32,
             )
@@ -244,14 +276,14 @@
     halo_start(eg, 2)
     halo_wait_recv(eg, 2)
     build(eg, sg)
-    gh[...] = conv(w2b, sg)
-
-    for st in range(2):
+    gh[...] = conv_back(w2b, sg)
+
+    for st in range(3):
         local_copy(st).wait()
-    bases = [0, 0]
+    bases = [0, 0, 0]
     for t in range(steps):
         n = devices >> (t + 1)
-        for st in range(2):
+        for st in range(3):
             rs_copy(st, t).wait_recv()
             if t == 0:
                 def fold(i, carry, st=st):
@@ -260,8 +292,11 @@
             else:
                 bases[st] = bases[st] + my_bit(orders[st], t) * n
 
-                def fold(i, carry, st=st, base=bases[st], off=offs[t]):
-                    acc[st, base + i] = acc[st, base + i] + recv[st, off + i].astype(F32)
+                got = recv if t < 2 else recv32
+                begin = offs[t] if t < 2 else offs[t] - offs[2]
+
+                def fold(i, carry, st=st, base=bases[st], off=begin, got=got):
+                    acc[st, base + i] = acc[st, base + i] + got[st, off + i].astype(F32)
                     return carry
             lax.fori_loop(0, n, fold, 0)
             if t + 1 < steps:
@@ -271,16 +306,18 @@
                 def put(i, carry, st=st, give=give, off=offs[t + 1] - half):
                     stage[st, off + i] = acc[st, give + i].astype(BF)
                     return carry
-                lax.fori_loop(0, m, put, 0)
+                if t + 1 < 2:
+                    lax.fori_loop(0, m, put, 0)
                 rs_copy(st, t + 1).start()
-    for st in range(2):
-        for b in range(2):
-            lo = (2 * st + b) * LANES
-            ev[st + 1, b + 1] = (live[:, lo : lo + LANES] * acc[st, bases[st], b]).astype(BF)
+    for st in range(3):
+        for b in range(4):
+            ev[1 + b // 2, 1 + b % 2, st * third : (st + 1) * third] = (
+                live[:, b * LANES : (b + 1) * LANES] * acc[st, bases[st], b]
+            ).astype(BF)
     halo_start(ev, 0)
     halo_wait_recv(ev, 0)
     build(ev, sv)
-    pre[...] = conv(w1f, sv)
+    pre[...] = conv(w1, sv)
     first = pre[...]
     sig = 1.0 / (1.0 + jnp.exp(-first))
     write_interior(eh, (live * first * sig).astype(BF))
@@ -293,15 +330,29 @@
     weight_part(1, sh, read_interior(eg))
     rb = wacc.shape[1] // devices
 
+    def w_base(c, t):
+        base = 0
+        for u in range(t):
+            base = base + my_bit(orders[c], u) * (devices >> (u + 1))
+        return base
+
     def ws_copy(c, t):
-        n = (devices >> (t + 1)) * rb
+        m = devices >> (t + 1)
+        n = m * rb
+        if t < 2:
+            src = wstage.at[c, pl.ds(offs[t] * rb, n)]
+            dst = wrecv.at[c, pl.ds(offs[t] * rb, n)]
+        else:
+            give = w_base(c, t) + (1 - my_bit(orders[c], t)) * m
+            src = wacc.at[c, pl.ds(pl.multiple_of(give * rb, 16), n)]
+            dst = wrecv32.at[c, pl.ds((offs[t] - offs[2]) * rb, n)]
         return pltpu.make_async_remote_copy(
-            src_ref=wstage.at[c, pl.ds(offs[t] * rb, n)], dst_ref=wrecv.at[c, pl.ds(offs[t] * rb, n)],
+            src_ref=src, dst_ref=dst,
             send_sem=ws_send.at[c, t], recv_sem=ws_recv.at[c, t],
             device_id=partner(*orders[c][t]), device_id_type=MESH,
         )
 
-    wbase = [0, 0]
+    wbase = [0, 0, 0]
 
     def ws_begin(c, t):
         m = devices >> (t + 1)
@@ -311,7 +362,8 @@
             wstage[c, pl.ds(pl.multiple_of((offs[t] + i) * rb, 16), rb)] = wacc[
                 c, pl.ds(pl.multiple_of((give + i) * rb, 16), rb)].astype(BF)
             return carry
-        lax.fori_loop(0, m, put, 0)
+        if t < 2:
+            lax.fori_loop(0, m, put, 0)
         ws_copy(c, t).start()
 
     def ws_finish(c, t):
@@ -319,30 +371,33 @@
         wbase[c] = wbase[c] + my_bit(orders[c], t) * m
         ws_copy(c, t).wait_recv()
         base = wbase[c]
+        got = wrecv if t < 2 else wrecv32
+        begin = offs[t] if t < 2 else offs[t] - offs[2]
 
         def fold(i, carry):
             at = pl.ds(pl.multiple_of((base + i) * rb, 16), rb)
-            wacc[c, at] = wacc[c, at] + wrecv[
-                c, pl.ds(pl.multiple_of((offs[t] + i) * rb, 16), rb)].astype(F32)
+            wacc[c, at] = wacc[c, at] + got[
+                c, pl.ds(pl.multiple_of((begin + i) * rb, 16), rb)].astype(F32)
             return carry
         lax.fori_loop(0, m, fold, 0)
 
-    for c in range(2):
+    for c in range(3):
         ws_begin(c, 0)
     halo_wait_recv(ef, 3)
     build(ef, sg)
-    cells = (live * conv(w1b, sg)).astype(BF)
-    spots = [position(orders[st], g, s) for st in range(2)]
+    cells = (live * conv_back(w1b, sg)).astype(BF)
+    spots = [position(orders[st], g, s) for st in range(3)]
 
     def own_copy(st):
         return pltpu.make_async_copy(
             cells_buf.at[st], cells_out.at[st, spots[st]], own_sem.at[st]
         )
 
-    for st in range(2):
-        for b in range(2):
-            lo = (2 * st + b) * LANES
-            cells_buf[st, b] = cells[:, lo : lo + LANES]
+    for st in range(3):
+        for b in range(4):
+            cells_buf[st, b] = cells[
+                st * third : (st + 1) * third, b * LANES : (b + 1) * LANES
+            ]
         own_copy(st).start()
 
     def ag_copy(st, t):
@@ -365,16 +420,16 @@
             device_id=partner(*orders[st][steps - 1 - t]), device_id_type=MESH,
         ).wait_recv()
 
-    for st in range(2):
+    for st in range(3):
         own_copy(st).wait()
         ag_copy(st, 0).start()
-    out_field[...] = (live * conv(w2f, sh)).astype(BF)
+    out_field[...] = (live * conv(w2, sh)).astype(BF)
     for t in range(steps):
-        for st in range(2):
+        for st in range(3):
             ag_wait_recv(st, t)
             if t + 1 < steps:
                 ag_copy(st, t + 1).start()
-        for c in range(2):
+        for c in range(3):
             ws_finish(c, t)
             if t + 1 < steps:
                 ws_begin(c, t + 1)
@@ -391,13 +446,41 @@
             device_id=partner(*orders[c][steps - 1 - t]), device_id_type=MESH,
         )
 
-    for c in range(2):
+    def fetch(st):
+        return pltpu.make_async_copy(cells_out.at[st], recv.at[st], fetch_sem.at[st])
+
+    for st in range(3):
+        fetch(st).start()
+    for c in range(3):
         at = pl.ds(pl.multiple_of(spots[c] * rb, 16), rb)
         wall[c, at] = (wacc[c, at] * factor).astype(BF)
         wg_copy(c, 0).start()
+    for st in range(3):
+        fetch(st).wait()
+    rows = rows_out.shape[0]
+    group = 2
+    chunks = rows // group
+
+    def pick_rows(q, carry):
+        for u in range(group):
+            r = q * group + u
+            at = [spot[st, r] for st in range(3)]
+            full = jnp.concatenate(
+                [
+                    jnp.concatenate([recv[st, at[st], b] for b in range(4)], axis=1)
+                    for st in range(3)
+                ],
+                axis=0,
+            )
+            rows_out[r] = jnp.dot(
+                full, one_hot(places[r]), preferred_element_type=F32
+            ).astype(BF)
+        return carry
+
     for t in range(steps):
         n = 1 << t
-        for c in range(2):
+        lax.fori_loop(chunks * t // steps, chunks * (t + 1) // steps, pick_rows, 0)
+        for c in range(3):
             mine = spots[c] // n
             there = wg_ref(c, (mine + 1 - 2 * (mine % 2)) * n, n)
             pltpu.make_async_remote_copy(
@@ -407,10 +490,7 @@
             ).wait_recv()
             if t + 1 < steps:
                 wg_copy(c, t + 1).start()
-    gw1[...] = wall[0, :real_rows].astype(F32)
-    gw2[...] = wall[1, :real_rows].astype(F32)
-
-    for st in range(2):
+    for st in range(3):
         for t in range(steps):
             rs_copy(st, t).wait_send()
             ag_copy(st, t).wait_send()
@@ -432,92 +512,77 @@
     steps = len(orders[0])
     owner_g = row_owner // sa_count
     owner_s = row_owner % sa_count
-    place0 = position(orders[0], owner_g, owner_s)
-    place1 = position(orders[1], owner_g, owner_s)
-    is_live = jnp.arange(slot_len)[None, :] < row_count[:, None]
-    places = jnp.where(is_live, row_voxels, -1).reshape(row_total, 1, slot_len)
+    spot = jnp.stack([position(order, owner_g, owner_s) for order in orders])
+    is_live = jnp.arange(slot_len)[None, None, :] < row_count[:, None, None]
+    begins = (jnp.arange(slab_len) * plane_len)[None, :, None]
+    inner = row_voxels[:, None, :] - begins
+    places = jnp.where(is_live & (inner >= 0) & (inner < plane_len), inner, -1)
     feats = jnp.transpose(scan_feats, (1, 0, 2))
     vmem = pl.BlockSpec(memory_space=pltpu.VMEM)
     smem = pl.BlockSpec(memory_space=pltpu.SMEM)
     hbm = pl.BlockSpec(memory_space=pl.ANY)
-    grid_shape = (2, devices, 2, channels, LANES)
+    third = channels // 3
+    block = (4, third, LANES)
+    grid_shape = (3, devices) + block
     dense = pl.pallas_call(
         scatter_kernel,
         out_shape=jax.ShapeDtypeStruct(grid_shape, BF),
-        in_specs=[smem, smem, vmem, vmem],
+        in_specs=[smem, vmem, vmem],
         out_specs=vmem,
         scratch_shapes=[pltpu.VMEM(grid_shape, F32)],
         compiler_params=pltpu.CompilerParams(vmem_limit_bytes=VMEM_LIMIT),
         name="scatter_rows",
-    )(place0, place1, feats, places)
-
-    def forward(weight):
-        return jnp.transpose(weight.reshape(3, 9 * channels, channels), (0, 2, 1))
-
-    def backward(weight):
-        back = weight[::-1].reshape(3, 9, channels, channels)
-        return jnp.transpose(back, (0, 2, 1, 3)).reshape(3, channels, 9 * channels)
-
-    real_rows = 27 * channels
-    rb = -(-real_rows // (devices * 16)) * 16
+    )(spot, feats, places)
+
+    part_rows = 9 * channels
+    rb = -(-2 * part_rows // (devices * 16)) * 16
     wrows = rb * devices
     half = devices // 2
-    block = (2, channels, LANES)
     field = pltpu.VMEM((4, 4, channels, LANES), BF)
     stacked = pltpu.VMEM((9 * channels, 8 * LANES), BF)
     plane = pltpu.VMEM((channels, cell_total), F32)
+    turned = pltpu.VMEM((3, channels, 9 * channels), BF)
     dma = pltpu.SemaphoreType.DMA
     factor = 1.0 / math.sqrt(cell_total * devices)
-    out_field, cells, gw1, gw2 = pl.pallas_call(
+    out_field, cells, rows_out, wall = pl.pallas_call(
         functools.partial(main_kernel, gx_count, sa_count, factor),
         out_shape=(
             jax.ShapeDtypeStruct((channels, cell_total), BF),
             jax.ShapeDtypeStruct(grid_shape, BF),
-            jax.ShapeDtypeStruct((real_rows, channels), F32),
-            jax.ShapeDtypeStruct((real_rows, channels), F32),
+            jax.ShapeDtypeStruct((row_total, channels, slot_len), BF),
+            jax.ShapeDtypeStruct((3, wrows, channels), BF),
         ),
-        in_specs=[hbm] + [vmem] * 6,
+        in_specs=[smem, hbm] + [vmem] * 5,
         out_specs=(vmem, hbm, vmem, vmem),
         scratch_shapes=[
-            field, field, field, field, stacked, stacked, stacked, plane, plane,
-            pltpu.VMEM((2, half) + block, F32),
-            pltpu.VMEM((2, half) + block, BF),
-            pltpu.VMEM((2, devices) + block, BF),
-            pltpu.VMEM((2,) + block, BF),
-            pltpu.VMEM((2, wrows, channels), F32),
-            pltpu.VMEM((2, wrows, channels), BF),
-            pltpu.VMEM((2, wrows, channels), BF),
-            pltpu.VMEM((2, wrows, channels), BF),
-            dma((2,)), dma((2,)), dma((4, 8)), dma((4, 8)),
-            dma((2, steps)), dma((2, steps)), dma((2, steps)), dma((2, steps)),
-            dma((2, steps)), dma((2, steps)), dma((2, steps)), dma((2, steps)),
-        ],
+            field, field, field, field, stacked, stacked, stacked, plane, plane, turned, turned,
+            pltpu.VMEM((3, half) + block, F32),
+            pltpu.VMEM((3, half) + block, BF),
+            pltpu.VMEM(grid_shape, BF),
+            pltpu.VMEM((3, devices // 4) + block, F32),
+            pltpu.VMEM((3,) + block, BF),
+            pltpu.VMEM((3, wrows, channels), F32),
+            pltpu.VMEM((3, wrows * 3 // 4, channels), BF),
+            pltpu.VMEM((3, wrows * 3 // 4, channels), BF),
+            pltpu.VMEM((3, wrows // 4, channels), F32),
+            dma((3,)), dma((3,)), dma((3,)), dma((4, 8)), dma((4, 8)),
+        ] + [dma((3, steps))] * 8,
         compiler_params=pltpu.CompilerParams(
             collective_id=0, has_side_effects=True, vmem_limit_bytes=VMEM_LIMIT
         ),
         name="conv_pair",
     )(
+        spot,
         dense,
         occupancy.astype(F32).reshape(1, cell_total),
         cotangent.reshape(channels, cell_total),
-        forward(weight_one), forward(weight_two), backward(weight_one), backward(weight_two),
+        weight_one, weight_two, places,
     )
-    rows_out = pl.pallas_call(
-        gather_kernel,
-        out_shape=jax.ShapeDtypeStruct((row_total, channels, slot_len), BF),
-        in_specs=[smem, smem, vmem, vmem],
-        out_specs=vmem,
-        compiler_params=pltpu.CompilerParams(vmem_limit_bytes=VMEM_LIMIT),
-        name="gather_rows",
-    )(place0, place1, cells, places)
     grad_scan = jnp.transpose(rows_out, (1, 0, 2))
     weights = (27, channels, channels)
-    return (
-        out_field.reshape(channels, slab_len, plane_len),
-        grad_scan,
-        gw1.reshape(weights),
-        gw2.reshape(weights),
-    )
+    gw1 = wall[:, :part_rows].astype(F32).reshape(weights)
+    gw2 = wall[:, part_rows : 2 * part_rows].astype(F32).reshape(weights)
+    return (out_field.reshape(channels, slab_len, plane_len), grad_scan, gw1, gw2)
 
 
 def solution(mesh):

time: 158 us -> 131 us (0.83)
  Pallas kernels: 134 us -> 113 us
  local copies, waits for them, and re-layouts: 18.1 us -> 10.6 us
  other arithmetic: 4.01 us -> 6.67 us
    pallas_call x1 -> x0, Pallas kernels: 14.1 us -> none  [on_device(): pl.pallas_call(gather_kernel, out_shape=jax.ShapeDtypeStruct((row_total,...]
    pallas_call x1, Pallas kernels: 16.9 us -> 9.04 us  [on_device(): pl.pallas_call(scatter_kernel, out_shape=jax.ShapeDtypeStruct(grid_shape,...]
    reshape x6 -> x0, local copies, waits for them, and re-layouts: 6.03 us -> none  [the longest x2 3.2 us: forward(): return jnp.transpose(weight.reshape(3, 9 * channels, channels), (0, 2, 1))]
    reshape x0 -> x2, other arithmetic: none -> 2.42 us  [the longest x1 1.21 us: on_device(): gw1 = wall[:, :part_rows].astype(F32).reshape(weights)]
    add x2 -> x0, other arithmetic: 1.81 us -> none  [position(): place = place * 2 + bit_of(g if axis == 'gx' else s, bit)]
    unnamed x16 -> x6, local copies, waits for them, and re-layouts: 10.4 us -> 8.99 us
where the time goes in v2:
time: 131 us
  Pallas kernels  113 us (86%)
  local copies, waits for them, and re-layouts  10.6 us (8%)
  other arithmetic  6.67 us (5%)
    pallas_call x1, Pallas kernels, on_device(): pl.pallas_call(functools.partial(main_kernel, gx_count, sa_count, factor)...  104 us
    pallas_call x1, Pallas kernels, on_device(): pl.pallas_call(scatter_kernel, out_shape=jax.ShapeDtypeStruct(grid_shape,...  9.04 us
    unnamed x6, local copies, waits for them, and re-layouts  8.99 us

profile of v2, /device:TPU:0, one launch (start us, length us, event | category | flops | bytes accessed | tf_op | source)
XLA Modules:
  0.0 131.1 jit_solution(1137135097008875179)
XLA Ops:
  0.6 0.7 and_select_fusion.10
  1.3 0.7 convert_bitcast_fusion
  2.0 0.6 copy.14
  2.6 0.6 pad_add_fusion.spot
  3.2 0.7 iota_compare_fusion
  4.0 1.5 %and_select_fusion.places = s32[64,2,128]{2,1,0:T(2,128)} fusion(pred[64,128]{1,0:T(8,128)(4,1)S(1)} %iota_compare_fusion, s32[64,128]{1,0:T(8,128)} %param.10, s32[2]{0:T(128)S(1)} %iota_multiply_fusion), kind=kLoop, calls=%fused_computation.1 | loop fusion | flops 98304 | bytes 106504 | tf_op jit(solution)/shard_map/jit(_where)/select_n | solution.py:519
  5.5 1.5 %copy.15 = bf16[12,8,2,256]{3,1,2,0:T(8,128)(2,1)} copy(bf16[12,8,2,256]{3,2,1,0:T(2,128)(2,1)} %bitcast.25) | data formatting | bytes 196608
  7.0 3.6 %copy.17 = bf16[96,64,128]{2,0,1:T(8,128)(2,1)} copy(bf16[96,64,128]{2,1,0:T(8,128)(2,1)} %param.8) | data formatting | bytes 3145728 | tf_op args[0]
  10.6 9.0 %scatter_rows.1.dense = bf16[3,32,4,32,128]{4,3,2,1,0:T(8,128)(2,1)} custom-call(s32[3,64]{1,0:T(4,128)} %pad_add_fusion.spot, bf16[64,96,128]{2,1,0:T(8,128)(2,1)} %bitcast.20, s32[64,2,128]{2,1,0:T(2,128)} %and_select_fusion.places), custom_call_target="tpu_custom_call" | custom-call | tf_op jit(solution)/shard_map/scatter_rows/pallas_call | solution.py:527
  19.6 104.1 %conv_pair.1 = (bf16[96,512]{1,0:T(8,128)(2,1)}, bf16[3,32,4,32,128]{4,3,2,1,0:T(8,128)(2,1)}, bf16[64,96,128]{2,1,0:T(8,128)(2,1)}, bf16[3,2048,96]{2,1,0:T(8,128)(2,1)}) custom-call(s32[3,64]{1,0:T(4,128)} %pad_add_fusion.spot, bf16[3,32,4,32,128]{4,3,2,1,0:T(8,128)(2,1)} %scatter_rows.1.dense, f32[1,512]{1,0:T(1,128)} %bitcast.26, ...), custom_call_target="tpu_custom_call" | custom-call | tf_op jit(solution)/shard_map/conv_pair/pallas_call | solution.py:547
  123.7 1.6 %reshape.57 = bf16[96,2,256]{2,1,0:T(2,128)(2,1)} reshape(bf16[96,512]{1,0:T(8,128)(2,1)} %get-tuple-element.7) | data formatting | bytes 196608 | tf_op jit(solution)/shard_map/reshape | solution.py:585
  125.3 0.0 copy-start
  125.3 3.3 %copy.13 = bf16[96,64,128]{2,1,0:T(8,128)(2,1)} copy(bf16[96,64,128]{2,0,1:T(8,128)(2,1)} %bitcast.23) | data formatting | bytes 3145728
  128.6 0.0 copy-done
  128.6 0.1 fusion.5
  128.7 1.2 convert.2
  129.9 1.2 convert.3
  (3 shorter events, 0.0 us)
Async XLA Ops:
  125.3 3.3 %copy-start = (bf16[3,2048,96]{2,1,0:T(8,128)(2,1)S(1)}, bf16[3,2048,96]{2,1,0:T(8,128)(2,1)}, u32[]{:S(2)}) copy-start(bf16[3,2048,96]{2,1,0:T(8,128)(2,1)} %get-tuple-element.9) | copy-start | bytes 3538948

commit v3 on v2

--- a/solution.py
+++ b/solution.py
@@ -39,18 +39,23 @@
     return place
 
 
-def one_hot(places_pair):
-    both = places_pair.astype(F32).astype(BF)
-    cells = lax.broadcasted_iota(jnp.int32, (2 * LANES, both.shape[1]), 0)
+def one_hot(voxels, count):
+    slots = lax.broadcasted_iota(jnp.int32, voxels.shape, 1)
+    place = jnp.where(slots < count, voxels, -1)
+    cells = lax.broadcasted_iota(jnp.int32, (2 * LANES, voxels.shape[1]), 0)
     cells = cells.astype(F32).astype(BF)
     one = jnp.ones((), BF)
     zero = jnp.zeros((), BF)
     return jnp.concatenate(
-        [jnp.where(cells == both[p : p + 1], one, zero) for p in range(2)], axis=0
+        [
+            jnp.where(cells == (place - p * 2 * LANES).astype(F32).astype(BF), one, zero)
+            for p in range(2)
+        ],
+        axis=0,
     )
 
 
-def scatter_kernel(spot, feats, places, dense, total):
+def scatter_kernel(spot, owner, count, feats, voxels, dense, total):
     rows, channels, _ = feats.shape
     owners = dense.shape[1]
     third = channels // 3
@@ -68,14 +73,14 @@
             r = q * group + u
             parts.append(
                 lax.dot_general(
-                    feats[r], one_hot(places[r]), (((1,), (1,)), ((), ())),
+                    feats[r], one_hot(voxels[pl.ds(r, 1)], count[r]), (((1,), (1,)), ((), ())),
                     preferred_element_type=F32,
                 )
             )
         for u in range(group):
             r = q * group + u
             for st in range(3):
-                at = spot[st, r]
+                at = spot[st, owner[r]]
                 for b in range(4):
                     total[st, at, b] += parts[u][
                         st * third : (st + 1) * third, b * LANES : (b + 1) * LANES
@@ -93,7 +98,7 @@
 
 def main_kernel(
     gx_count, sa_count, factor,
-    spot, dense, occ, cot, w1, w2, places,
+    spot, owner, count, dense, occ, cot, w1, w2, voxels,
     out_field, cells_out, rows_out, wall,
     ev, eh, eg, ef, sv, sh, sg, pre, gh, w1b, w2b,
     acc, stage, recv, recv32, cells_buf, wacc, wstage, wrecv, wrecv32,
@@ -185,15 +190,18 @@
             base = base + my_bit(orders[st], u) * (devices >> (u + 1))
         return base
 
+    def narrow(t):
+        return t < 2 or t == steps - 1
+
     def rs_copy(st, t):
         n = devices >> (t + 1)
         if t == 0:
             src = dense.at[st, pl.ds((1 - my_bit(orders[st], 0)) * half, half)]
-        elif t < 2:
+        elif narrow(t):
             src = stage.at[st, pl.ds(offs[t] - half, n)]
         else:
             src = acc.at[st, pl.ds(rs_base(st, t) + (1 - my_bit(orders[st], t)) * n, n)]
-        if t < 2:
+        if narrow(t):
             dst = recv.at[st, pl.ds(offs[t], n)]
         else:
             dst = recv32.at[st, pl.ds(offs[t] - offs[2], n)]
@@ -292,8 +300,8 @@
             else:
                 bases[st] = bases[st] + my_bit(orders[st], t) * n
 
-                got = recv if t < 2 else recv32
-                begin = offs[t] if t < 2 else offs[t] - offs[2]
+                got = recv if narrow(t) else recv32
+                begin = offs[t] if narrow(t) else offs[t] - offs[2]
 
                 def fold(i, carry, st=st, base=bases[st], off=begin, got=got):
                     acc[st, base + i] = acc[st, base + i] + got[st, off + i].astype(F32)
@@ -306,7 +314,7 @@
                 def put(i, carry, st=st, give=give, off=offs[t + 1] - half):
                     stage[st, off + i] = acc[st, give + i].astype(BF)
                     return carry
-                if t + 1 < 2:
+                if narrow(t + 1):
                     lax.fori_loop(0, m, put, 0)
                 rs_copy(st, t + 1).start()
     for st in range(3):
@@ -339,7 +347,7 @@
     def ws_copy(c, t):
         m = devices >> (t + 1)
         n = m * rb
-        if t < 2:
+        if narrow(t):
             src = wstage.at[c, pl.ds(offs[t] * rb, n)]
             dst = wrecv.at[c, pl.ds(offs[t] * rb, n)]
         else:
@@ -362,7 +370,7 @@
             wstage[c, pl.ds(pl.multiple_of((offs[t] + i) * rb, 16), rb)] = wacc[
                 c, pl.ds(pl.multiple_of((give + i) * rb, 16), rb)].astype(BF)
             return carry
-        if t < 2:
+        if narrow(t):
             lax.fori_loop(0, m, put, 0)
         ws_copy(c, t).start()
 
@@ -371,8 +379,8 @@
         wbase[c] = wbase[c] + my_bit(orders[c], t) * m
         ws_copy(c, t).wait_recv()
         base = wbase[c]
-        got = wrecv if t < 2 else wrecv32
-        begin = offs[t] if t < 2 else offs[t] - offs[2]
+        got = wrecv if narrow(t) else wrecv32
+        begin = offs[t] if narrow(t) else offs[t] - offs[2]
 
         def fold(i, carry):
             at = pl.ds(pl.multiple_of((base + i) * rb, 16), rb)
@@ -464,7 +472,7 @@
     def pick_rows(q, carry):
         for u in range(group):
             r = q * group + u
-            at = [spot[st, r] for st in range(3)]
+            at = [spot[st, owner[r]] for st in range(3)]
             full = jnp.concatenate(
                 [
                     jnp.concatenate([recv[st, at[st], b] for b in range(4)], axis=1)
@@ -473,7 +481,7 @@
                 axis=0,
             )
             rows_out[r] = jnp.dot(
-                full, one_hot(places[r]), preferred_element_type=F32
+                full, one_hot(voxels[pl.ds(r, 1)], count[r]), preferred_element_type=F32
             ).astype(BF)
         return carry
 
@@ -510,13 +518,10 @@
     devices = gx_count * sa_count
     orders = bit_orders(gx_count, sa_count)
     steps = len(orders[0])
-    owner_g = row_owner // sa_count
-    owner_s = row_owner % sa_count
-    spot = jnp.stack([position(order, owner_g, owner_s) for order in orders])
-    is_live = jnp.arange(slot_len)[None, None, :] < row_count[:, None, None]
-    begins = (jnp.arange(slab_len) * plane_len)[None, :, None]
-    inner = row_voxels[:, None, :] - begins
-    places = jnp.where(is_live & (inner >= 0) & (inner < plane_len), inner, -1)
+    table = [
+        [position(order, o // sa_count, o % sa_count) for o in range(devices)] for order in orders
+    ]
+    spot = jnp.asarray(table, jnp.int32)
     feats = jnp.transpose(scan_feats, (1, 0, 2))
     vmem = pl.BlockSpec(memory_space=pltpu.VMEM)
     smem = pl.BlockSpec(memory_space=pltpu.SMEM)
@@ -527,12 +532,12 @@
     dense = pl.pallas_call(
         scatter_kernel,
         out_shape=jax.ShapeDtypeStruct(grid_shape, BF),
-        in_specs=[smem, vmem, vmem],
+        in_specs=[smem, smem, smem, vmem, vmem],
         out_specs=vmem,
         scratch_shapes=[pltpu.VMEM(grid_shape, F32)],
         compiler_params=pltpu.CompilerParams(vmem_limit_bytes=VMEM_LIMIT),
         name="scatter_rows",
-    )(spot, feats, places)
+    )(spot, row_owner, row_count, feats, row_voxels)
 
     part_rows = 9 * channels
     rb = -(-2 * part_rows // (devices * 16)) * 16
@@ -552,7 +557,7 @@
             jax.ShapeDtypeStruct((row_total, channels, slot_len), BF),
             jax.ShapeDtypeStruct((3, wrows, channels), BF),
         ),
-        in_specs=[smem, hbm] + [vmem] * 5,
+        in_specs=[smem, smem, smem, hbm] + [vmem] * 5,
         out_specs=(vmem, hbm, vmem, vmem),
         scratch_shapes=[
             field, field, field, field, stacked, stacked, stacked, plane, plane, turned, turned,
@@ -562,8 +567,8 @@
             pltpu.VMEM((3, devices // 4) + block, F32),
             pltpu.VMEM((3,) + block, BF),
             pltpu.VMEM((3, wrows, channels), F32),
-            pltpu.VMEM((3, wrows * 3 // 4, channels), BF),
-            pltpu.VMEM((3, wrows * 3 // 4, channels), BF),
+            pltpu.VMEM((3, wrows, channels), BF),
+            pltpu.VMEM((3, wrows, channels), BF),
             pltpu.VMEM((3, wrows // 4, channels), F32),
             dma((3,)), dma((3,)), dma((3,)), dma((4, 8)), dma((4, 8)),
         ] + [dma((3, steps))] * 8,
@@ -573,10 +578,12 @@
         name="conv_pair",
     )(
         spot,
+        row_owner,
+        row_count,
         dense,
         occupancy.astype(F32).reshape(1, cell_total),
         cotangent.reshape(channels, cell_total),
-        weight_one, weight_two, places,
+        weight_one, weight_two, row_voxels,
     )
     grad_scan = jnp.transpose(rows_out, (1, 0, 2))
     weights = (27, channels, channels)

time: 131 us -> 122 us (0.931)
  Pallas kernels: 113 us -> 107 us
  other arithmetic: 6.67 us -> 3.11 us
    pallas_call x1, Pallas kernels: 104 us -> 98.3 us  [on_device(): pl.pallas_call(functools.partial(main_kernel, gx_count, sa_count, factor)...]
    select_n x2 -> x0, other arithmetic: 2.21 us -> none  [the longest x1 1.54 us: on_device(): places = jnp.where(is_live & (inner >= 0) & (inner < plane_len), inner, -1)]
where the time goes in v3:
time: 122 us
  Pallas kernels  107 us (88%)
  local copies, waits for them, and re-layouts  10.6 us (9%)
  other arithmetic  3.11 us (3%)
    pallas_call x1, Pallas kernels, on_device(): pl.pallas_call(functools.partial(main_kernel, gx_count, sa_count, factor)...  98.3 us
    pallas_call x1, Pallas kernels, on_device(): pl.pallas_call(scatter_kernel, out_shape=jax.ShapeDtypeStruct(grid_shape,...  9.1 us
    unnamed x6, local copies, waits for them, and re-layouts  8.97 us

profile of v3, /device:TPU:0, one launch (start us, length us, event | category | flops | bytes accessed | tf_op | source)
XLA Modules:
  0.0 121.8 jit_solution(1990187114638319321)
XLA Ops:
  0.6 0.7 convert_bitcast_fusion
  1.3 0.6 copy.15
  1.9 1.5 %copy.16 = bf16[12,8,2,256]{3,1,2,0:T(8,128)(2,1)} copy(bf16[12,8,2,256]{3,2,1,0:T(2,128)(2,1)} %bitcast.19) | data formatting | bytes 196608
  3.4 3.6 %copy.18 = bf16[96,64,128]{2,0,1:T(8,128)(2,1)} copy(bf16[96,64,128]{2,1,0:T(8,128)(2,1)} %param.9) | data formatting | bytes 3145728 | tf_op args[0]
  7.0 9.1 %scatter_rows.1.dense = bf16[3,32,4,32,128]{4,3,2,1,0:T(8,128)(2,1)} custom-call(s32[3,32]{1,0:T(4,128)} %constant.2.clone.spot, s32[64]{0:T(128)} %owner.3, s32[64]{0:T(128)} %count.3, bf16[64,96,128]{2,1,0:T(8,128)(2,1)} %bitcast.14, s32[64,128]{1,0:T(8,128)} %voxels.3), custom_call_target="tpu_custom_call" | custom-call | tf_op jit(solution)/shard_map/scatter_rows/pallas_call | solution.py:532
  16.1 98.3 %conv_pair.1 = (bf16[96,512]{1,0:T(8,128)(2,1)}, bf16[3,32,4,32,128]{4,3,2,1,0:T(8,128)(2,1)}, bf16[64,96,128]{2,1,0:T(8,128)(2,1)}, bf16[3,2048,96]{2,1,0:T(8,128)(2,1)}) custom-call(s32[3,32]{1,0:T(4,128)} %constant.2.clone.spot, s32[64]{0:T(128)} %owner.3, s32[64]{0:T(128)} %count.3, bf16[3,32,4,32,128]{4,3,2,1,0:T(8,128)(2,1)} %scatter_rows.1.dense, ...), custom_call_target="tpu_custom_call" | custom-call | tf_op jit(solution)/shard_map/conv_pair/pallas_call | solution.py:552
  114.5 1.6 %reshape.31 = bf16[96,2,256]{2,1,0:T(2,128)(2,1)} reshape(bf16[96,512]{1,0:T(8,128)(2,1)} %get-tuple-element.7) | data formatting | bytes 196608 | tf_op jit(solution)/shard_map/reshape | solution.py:592
  116.0 0.0 copy-start
  116.0 3.3 %copy.14 = bf16[96,64,128]{2,1,0:T(8,128)(2,1)} copy(bf16[96,64,128]{2,0,1:T(8,128)(2,1)} %bitcast.17) | data formatting | bytes 3145728
  119.3 0.0 copy-done
  119.3 0.1 fusion
  119.4 1.2 convert.2
  120.6 1.2 convert.3
Async XLA Ops:
  116.0 3.3 %copy-start = (bf16[3,2048,96]{2,1,0:T(8,128)(2,1)S(1)}, bf16[3,2048,96]{2,1,0:T(8,128)(2,1)}, u32[]{:S(2)}) copy-start(bf16[3,2048,96]{2,1,0:T(8,128)(2,1)} %get-tuple-element.9) | copy-start | bytes 3538948
